TPU v7x, 256 devices: a whole 4x4x8 slice. The times are simulated.
256 devices in a mesh: ctx: 64 (over y, z_hi, x), head: 4 (over z_lo, core).
Axes of the slice: x: 4, y: 4, z: 8 (z_hi: 4, z_lo: 2; z = z_hi * 2 + z_lo), core: 2. Of those that a mesh axis runs over, the one named last changes fastest.
Arguments:
- long_qkv: bfloat16 [3, 8192, 5120], P(None, 'ctx', 'head'), may hold values from -640 to 640
- long_grad: bfloat16 [8192, 5120], P('ctx', 'head'), may hold values from -24 to 24
- short_qkv: bfloat16 [3, 8192, 5120], P(None, 'ctx', 'head'), may hold values from -640 to 640
- short_grad: bfloat16 [8192, 5120], P('ctx', 'head'), may hold values from -24 to 24
- short_lengths: int32 [256], replicated, may hold values from 1 to 64, 8192 in all
- norm_gains: float32 [2, 5120], P(None, 'head'), may hold values from 0.25 to 1.75
Outputs:
- long_out: bfloat16 [8192, 5120], P('ctx', 'head')
- long_dqkv: bfloat16 [3, 8192, 5120], P(None, 'ctx', 'head')
- short_out: bfloat16 [8192, 5120], P('ctx', 'head')
- short_dqkv: bfloat16 [3, 8192, 5120], P(None, 'ctx', 'head')
Inputs may be any that keep to these rules, and one draw needn't show every extreme that they name: `short_lengths`: the 256 short documents lie end to end in this order over the 8192 short tokens.
All inputs are finite; a program needn't handle non-finite values.
Results may differ from a plain program's by a relative error of at most 0.012.
The roundings to bfloat16 on the way count: a program that leaves them out, or rounds other values in their place, can miss the bound.
Values may be sent and summed in bfloat16 or wider, within the bound.
A program may use at most 128 MiB of HBM per device.

v0:
```python
import jax
import jax.numpy as jnp
from jax import lax
from jax.sharding import PartitionSpec as P

HEAD_DIM = 128
SPAN = 8
WIDTH = 5120
DOC_MAX = 64


EPSILON = 1e-06
NEGATIVE = -1e30


def passed_along(shard, axis, by):
    size = lax.axis_size(axis)
    pairs = [(i, i + by) for i in range(size) if 0 <= i + by < size]
    return lax.ppermute(shard, axis, pairs)


def by_heads(matrix):
    return matrix.reshape(matrix.shape[0], -1, HEAD_DIM)


def square_sum(matrix):
    widened = matrix.astype(jnp.float32)
    return jnp.sum(widened * widened, axis=1)


def inner_sum(matrix, gain_row, gradient):
    return jnp.sum(gradient * gain_row * matrix.astype(jnp.float32), axis=1)


def normalize(matrix, gain_row, running):
    widened = matrix.astype(jnp.float32)
    inverse = lax.rsqrt(running[:, None] / WIDTH + EPSILON)
    return ((widened * inverse * gain_row).astype(jnp.bfloat16), inverse)


def norm_back(matrix, gain_row, inverse, gradient, inner_total):
    widened = matrix.astype(jnp.float32)
    return (
        inverse * gain_row * gradient
        - widened * (inverse * inverse * inverse) * inner_total[:, None] / WIDTH
    ).astype(jnp.bfloat16)


def block_scores(query_heads, key_heads, allowed):
    factor = HEAD_DIM ** (-0.5)
    raw_scores = (
        jnp.einsum("qhd,khd->hqk", query_heads, key_heads, preferred_element_type=jnp.float32)
        * factor
    )
    return jnp.where(allowed[None], raw_scores, NEGATIVE)


def block_stats(query_heads, key_heads, allowed, highest, running):
    scores = block_scores(query_heads, key_heads, allowed)
    newest = jnp.maximum(highest, jnp.max(scores, axis=2))
    return (
        newest,
        running * jnp.exp(highest - newest) + jnp.sum(jnp.exp(scores - newest[:, :, None]), axis=2),
    )


def block_mix(query_heads, key_heads, value_heads, allowed, log_total, mixed_sum):
    scores = block_scores(query_heads, key_heads, allowed)
    weights = jnp.exp(scores - log_total[:, :, None]).astype(jnp.bfloat16)
    return mixed_sum + jnp.einsum(
        "hqk,khd->qhd", weights, value_heads, preferred_element_type=jnp.float32
    )


def block_back(query_heads, grad_heads, key_heads, value_heads, allowed, log_total, row_dot):
    factor = HEAD_DIM ** (-0.5)
    scores = block_scores(query_heads, key_heads, allowed)
    probability = jnp.exp(scores - log_total[:, :, None])
    weights = probability.astype(jnp.bfloat16)
    weight_grad = jnp.einsum(
        "qhd,khd->hqk", grad_heads, value_heads, preferred_element_type=jnp.float32
    )
    score_grad = (probability * (weight_grad - row_dot[:, :, None])).astype(jnp.bfloat16)
    query_part = (
        jnp.einsum("hqk,khd->qhd", score_grad, key_heads, preferred_element_type=jnp.float32)
        * factor
    )
    key_part = (
        jnp.einsum("hqk,qhd->khd", score_grad, query_heads, preferred_element_type=jnp.float32)
        * factor
    )
    value_part = jnp.einsum("hqk,qhd->khd", weights, grad_heads, preferred_element_type=jnp.float32)
    return (query_part, key_part, value_part)


def mask_for(offset, position, causal):
    return causal if offset == 0 else jnp.broadcast_to(offset <= position, causal.shape)


def segment_of(positions, doc_ends):
    counted = jnp.sum(
        (positions[:, None] >= doc_ends[None, :]).astype(jnp.int32), axis=1, dtype=jnp.int32
    )
    return jnp.where(positions >= 0, counted, -1)


def row_dots(grad_heads, output):
    return jnp.sum(grad_heads.astype(jnp.float32) * by_heads(output).astype(jnp.float32), axis=2).T


def on_device(long_qkv, long_grad, short_qkv, short_grad, short_lengths, norm_gains):
    long_rows = long_qkv.shape[1]
    short_rows = short_qkv.shape[1]
    sources = (long_qkv[0], long_qkv[1], short_qkv[0], short_qkv[1])
    gains = (norm_gains[0], norm_gains[1], norm_gains[0], norm_gains[1])
    totals = lax.psum(
        (
            square_sum(sources[0]),
            square_sum(sources[1]),
            square_sum(sources[2]),
            square_sum(sources[3]),
        ),
        "head",
    )
    normalized = [normalize(sources[slot], gains[slot], totals[slot]) for slot in range(4)]
    position = lax.axis_index("ctx") % SPAN
    long_q = normalized[0][0]
    long_k = normalized[1][0]
    long_v = long_qkv[2]
    query_heads = by_heads(long_q)
    grad_heads = by_heads(long_grad)
    head_count = query_heads.shape[1]
    blocks = [(long_k, long_v)]
    current = (long_k, long_v)
    for offset in range(1, SPAN):
        current = passed_along((current[0], current[1]), "ctx", 1)
        blocks.append(current)
    causal = jnp.arange(long_rows)[:, None] >= jnp.arange(long_rows)[None, :]
    highest = jnp.full((head_count, long_rows), NEGATIVE, jnp.float32)
    running = jnp.zeros((head_count, long_rows), jnp.float32)
    for offset in range(SPAN):
        allowed = mask_for(offset, position, causal)
        highest, running = block_stats(
            query_heads, by_heads(blocks[offset][0]), allowed, highest, running
        )
    log_total = highest + jnp.log(running)
    mixed_sum = jnp.zeros((long_rows, head_count, HEAD_DIM), jnp.float32)
    for offset in range(SPAN):
        allowed = mask_for(offset, position, causal)
        mixed_sum = block_mix(
            query_heads,
            by_heads(blocks[offset][0]),
            by_heads(blocks[offset][1]),
            allowed,
            log_total,
            mixed_sum,
        )
    long_out = mixed_sum.reshape(long_rows, -1).astype(jnp.bfloat16)
    long_row_dot = row_dots(grad_heads, long_out)
    empty = jnp.zeros((long_rows, head_count, HEAD_DIM), jnp.float32)
    query_total = empty
    carried = (empty, empty)
    for offset in reversed(range(SPAN)):
        allowed = mask_for(offset, position, causal)
        query_part, key_part, value_part = block_back(
            query_heads,
            grad_heads,
            by_heads(blocks[offset][0]),
            by_heads(blocks[offset][1]),
            allowed,
            log_total,
            long_row_dot,
        )
        query_total = query_total + query_part
        if offset == SPAN - 1:
            carried = (key_part, value_part)
        else:
            arrived = passed_along((carried[0], carried[1]), "ctx", -1)
            carried = (arrived[0] + key_part, arrived[1] + value_part)
    key_total, value_total = carried
    short_q = normalized[2][0]
    short_k = normalized[3][0]
    short_v = short_qkv[2]
    rim_k, rim_v = passed_along(
        (short_k[short_rows - DOC_MAX :], short_v[short_rows - DOC_MAX :]), "ctx", 1
    )
    short_keys = by_heads(jnp.concatenate([rim_k, short_k], axis=0))
    short_values = by_heads(jnp.concatenate([rim_v, short_v], axis=0))
    ctx_index = lax.axis_index("ctx")
    doc_ends = jnp.cumsum(short_lengths, dtype=jnp.int32)
    first_row = ctx_index * short_rows
    query_pos = first_row + jnp.arange(short_rows, dtype=jnp.int32)
    key_pos = first_row - DOC_MAX + jnp.arange(short_rows + DOC_MAX, dtype=jnp.int32)
    query_seg = segment_of(query_pos, doc_ends)
    key_seg = segment_of(key_pos, doc_ends)
    short_allowed = (query_seg[:, None] == key_seg[None, :]) & (
        key_pos[None, :] <= query_pos[:, None]
    )
    short_heads = by_heads(short_q)
    short_grad_heads = by_heads(short_grad)
    short_scores = block_scores(short_heads, short_keys, short_allowed)
    short_high = jnp.max(short_scores, axis=2, keepdims=True)
    short_log = short_high[:, :, 0] + jnp.log(jnp.sum(jnp.exp(short_scores - short_high), axis=2))
    short_mixed = block_mix(
        short_heads,
        short_keys,
        short_values,
        short_allowed,
        short_log,
        jnp.zeros((short_rows, head_count, HEAD_DIM), jnp.float32),
    )
    short_out = short_mixed.reshape(short_rows, -1).astype(jnp.bfloat16)
    short_query, short_key_part, short_value_part = block_back(
        short_heads,
        short_grad_heads,
        short_keys,
        short_values,
        short_allowed,
        short_log,
        row_dots(short_grad_heads, short_out),
    )
    back_k, back_v = passed_along((short_key_part[:DOC_MAX], short_value_part[:DOC_MAX]), "ctx", -1)
    own_k = short_key_part[DOC_MAX:]
    own_v = short_value_part[DOC_MAX:]
    short_key_total = jnp.concatenate(
        [own_k[: short_rows - DOC_MAX], own_k[short_rows - DOC_MAX :] + back_k], axis=0
    )
    short_value_total = jnp.concatenate(
        [own_v[: short_rows - DOC_MAX], own_v[short_rows - DOC_MAX :] + back_v], axis=0
    )
    gradients = (
        query_total.reshape(long_rows, -1),
        key_total.reshape(long_rows, -1),
        short_query.reshape(short_rows, -1),
        short_key_total.reshape(short_rows, -1),
    )
    inners = lax.psum(
        (
            inner_sum(sources[0], gains[0], gradients[0]),
            inner_sum(sources[1], gains[1], gradients[1]),
            inner_sum(sources[2], gains[2], gradients[2]),
            inner_sum(sources[3], gains[3], gradients[3]),
        ),
        "head",
    )
    results = [
        norm_back(sources[slot], gains[slot], normalized[slot][1], gradients[slot], inners[slot])
        for slot in range(4)
    ]
    long_dqkv = jnp.stack(
        [results[0], results[1], value_total.reshape(long_rows, -1).astype(jnp.bfloat16)]
    )
    short_dqkv = jnp.stack(
        [results[2], results[3], short_value_total.reshape(short_rows, -1).astype(jnp.bfloat16)]
    )
    return (long_out, long_dqkv, short_out, short_dqkv)


def solution(mesh):
    return jax.shard_map(
        on_device,
        mesh=mesh,
        in_specs=(
            P(None, "ctx", "head"),
            P("ctx", "head"),
            P(None, "ctx", "head"),
            P("ctx", "head"),
            P(),
            P(None, "head"),
        ),
        out_specs=(
            P("ctx", "head"),
            P(None, "ctx", "head"),
            P("ctx", "head"),
            P(None, "ctx", "head"),
        ),
        check_vma=False,
    )
```

profile of v0, /device:TPU:86, one launch (start us, length us, event | category | flops | bytes accessed | tf_op | source)
XLA Modules:
  0.0 675.7 jit_solution(14832266209877698662)
XLA Ops:
  0.6 2.0 slice_bitcast_fusion.1
  5.5 7.3 %all-reduce.1 = (f32[128]{0:T(128)S(1)}, f32[128]{0:T(128)S(1)}, f32[128]{0:T(128)S(1)}, f32[128]{0:T(128)S(1)}) all-reduce(f32[128]{0:T(128)S(1)} %multiply_reduce_fusion.5, f32[128]{0:T(128)S(1)} %fusion.66, f32[128]{0:T(128)S(1)} %fusion.51, f32[128]{0:T(128)S(1)} %multiply_reduce_fusion.1), channel_id=1, replica_groups=mesh['ctx'=64,'head'=4] {'head'}, use_global_device_ids=true, to_apply=%region_1.0 | all-reduce | flops 512 | bytes 4096 | tf_op jit(solution)/shard_map/psum | solution.py:116
  13.8 5.4 collective-permute-start
  19.2 3.4 collective-permute-start.7
  23.5 3.4 collective-permute-start.29
  28.5 3.1 collective-permute-start.28
  38.4 11.6 %collective-permute-done.29 = bf16[64,1280]{0,1:T(8,128)(2,1)} collective-permute-done((bf16[64,1280]{0,1:T(8,128)(2,1)}, bf16[64,1280]{0,1:T(8,128)(2,1)}, u32[]{:S(2)}, u32[]{:S(2)}) %collective-permute-start.29) | collective-permute-done | bytes 163872 | tf_op jit(solution)/shard_map/ppermute | solution.py:19
  51.9 15.9 %collective-permute-done.28 = bf16[64,1280]{1,0:T(8,128)(2,1)S(1)} collective-permute-done((bf16[64,1280]{1,0:T(8,128)(2,1)}, bf16[64,1280]{1,0:T(8,128)(2,1)S(1)}, u32[]{:S(2)}, u32[]{:S(2)}) %collective-permute-start.28) | collective-permute-done | bytes 163872 | tf_op jit(solution)/shard_map/ppermute | solution.py:19
  70.8 1.9 collective-permute-start.30
  73.9 2.2 copy.362
  76.4 8.6 %collective-permute-start.1 = (bf16[128,1280]{0,1:T(8,128)(2,1)}, bf16[128,1280]{0,1:T(8,128)(2,1)}, u32[]{:S(2)}, u32[]{:S(2)}) collective-permute-start(bf16[128,1280]{0,1:T(8,128)(2,1)} %collective-permute-done), channel_id=1, source_target_pairs={{0,4},{4,8},{8,12},{12,16},{16,20},{20,24},{24,28},{28,32},{32,36}... | collective-permute-start | bytes 983048 | tf_op jit(solution)/shard_map/ppermute | solution.py:19
  85.1 3.9 collective-permute-start.8
  93.0 1.9 collective-permute-start.31
  98.2 9.3 %collective-permute-done.1 = bf16[128,1280]{0,1:T(8,128)(2,1)} collective-permute-done((bf16[128,1280]{0,1:T(8,128)(2,1)}, bf16[128,1280]{0,1:T(8,128)(2,1)}, u32[]{:S(2)}, u32[]{:S(2)}) %collective-permute-start.1) | collective-permute-done | bytes 327712 | tf_op jit(solution)/shard_map/ppermute | solution.py:19
  107.4 8.7 %collective-permute-start.2 = (bf16[128,1280]{0,1:T(8,128)(2,1)}, bf16[128,1280]{0,1:T(8,128)(2,1)S(1)}, u32[]{:S(2)}, u32[]{:S(2)}) collective-permute-start(bf16[128,1280]{0,1:T(8,128)(2,1)} %collective-permute-done.1), channel_id=1, source_target_pairs={{0,4},{4,8},{8,12},{12,16},{16,20},{20,24},{24,28},{28,32},{32,36}... | collective-permute-start | bytes 983048 | tf_op jit(solution)/shard_map/ppermute | solution.py:19
  116.1 6.3 collective-permute-start.9
  125.5 2.2 copy.364
  127.8 3.0 collective-permute-done.2
  130.8 8.5 %collective-permute-start.3 = (bf16[128,1280]{0,1:T(8,128)(2,1)S(1)}, bf16[128,1280]{0,1:T(8,128)(2,1)}, u32[]{:S(2)}, u32[]{:S(2)}) collective-permute-start(bf16[128,1280]{0,1:T(8,128)(2,1)S(1)} %collective-permute-done.2), channel_id=1, source_target_pairs={{0,4},{4,8},{8,12},{12,16},{16,20},{20,24},{24,28},{28,32},{32,36}... | collective-permute-start | bytes 983048 | tf_op jit(solution)/shard_map/ppermute | solution.py:19
  140.9 8.0 %collective-permute-start.10 = (bf16[128,1280]{1,0:T(8,128)(2,1)}, bf16[128,1280]{1,0:T(8,128)(2,1)}, u32[]{:S(2)}, u32[]{:S(2)}) collective-permute-start(bf16[128,1280]{1,0:T(8,128)(2,1)} %collective-permute-done.9), channel_id=1, source_target_pairs={{0,4},{4,8},{8,12},{12,16},{16,20},{20,24},{24,28},{28,32},{32,36}... | collective-permute-start | bytes 983048 | tf_op jit(solution)/shard_map/ppermute | solution.py:19
  150.0 2.3 collective-permute-done.3
  152.3 8.8 %collective-permute-start.4 = (bf16[128,1280]{0,1:T(8,128)(2,1)}, bf16[128,1280]{0,1:T(8,128)(2,1)S(1)}, u32[]{:S(2)}, u32[]{:S(2)}) collective-permute-start(bf16[128,1280]{0,1:T(8,128)(2,1)} %collective-permute-done.3), channel_id=1, source_target_pairs={{0,4},{4,8},{8,12},{12,16},{16,20},{20,24},{24,28},{28,32},{32,36}... | collective-permute-start | bytes 983048 | tf_op jit(solution)/shard_map/ppermute | solution.py:19
  163.1 8.8 %collective-permute-start.11 = (bf16[128,1280]{1,0:T(8,128)(2,1)}, bf16[128,1280]{1,0:T(8,128)(2,1)}, u32[]{:S(2)}, u32[]{:S(2)}) collective-permute-start(bf16[128,1280]{1,0:T(8,128)(2,1)} %collective-permute-done.10), channel_id=1, source_target_pairs={{0,4},{4,8},{8,12},{12,16},{16,20},{20,24},{24,28},{28,32},{32,36}... | collective-permute-start | bytes 983048 | tf_op jit(solution)/shard_map/ppermute | solution.py:19
  172.0 2.2 fusion.110
  174.2 1.9 copy.260
  176.1 8.6 %collective-permute-start.5 = (bf16[128,1280]{0,1:T(8,128)(2,1)S(1)}, bf16[128,1280]{0,1:T(8,128)(2,1)}, u32[]{:S(2)}, u32[]{:S(2)}) collective-permute-start(bf16[128,1280]{0,1:T(8,128)(2,1)S(1)} %collective-permute-done.4), channel_id=1, source_target_pairs={{0,4},{4,8},{8,12},{12,16},{16,20},{20,24},{24,28},{28,32},{32,36}... | collective-permute-start | bytes 983048 | tf_op jit(solution)/shard_map/ppermute | solution.py:19
  186.9 16.1 %collective-permute-done.11 = bf16[128,1280]{1,0:T(8,128)(2,1)} collective-permute-done((bf16[128,1280]{1,0:T(8,128)(2,1)}, bf16[128,1280]{1,0:T(8,128)(2,1)}, u32[]{:S(2)}, u32[]{:S(2)}) %collective-permute-start.11) | collective-permute-done | bytes 327712 | tf_op jit(solution)/shard_map/ppermute | solution.py:19
  203.0 8.8 %collective-permute-start.12 = (bf16[128,1280]{1,0:T(8,128)(2,1)}, bf16[128,1280]{1,0:T(8,128)(2,1)}, u32[]{:S(2)}, u32[]{:S(2)}) collective-permute-start(bf16[128,1280]{1,0:T(8,128)(2,1)} %collective-permute-done.11), channel_id=1, source_target_pairs={{0,4},{4,8},{8,12},{12,16},{16,20},{20,24},{24,28},{28,32},{32,36}... | collective-permute-start | bytes 983048 | tf_op jit(solution)/shard_map/ppermute | solution.py:19
  211.9 2.2 fusion.108
  214.1 1.9 copy.264
  216.0 9.3 %collective-permute-done.5 = bf16[128,1280]{0,1:T(8,128)(2,1)} collective-permute-done((bf16[128,1280]{0,1:T(8,128)(2,1)S(1)}, bf16[128,1280]{0,1:T(8,128)(2,1)}, u32[]{:S(2)}, u32[]{:S(2)}) %collective-permute-start.5) | collective-permute-done | bytes 327712 | tf_op jit(solution)/shard_map/ppermute | solution.py:19
  225.2 12.6 %collective-permute-start.6 = (bf16[128,1280]{0,1:T(8,128)(2,1)}, bf16[128,1280]{0,1:T(8,128)(2,1)S(1)}, u32[]{:S(2)}, u32[]{:S(2)}) collective-permute-start(bf16[128,1280]{0,1:T(8,128)(2,1)} %collective-permute-done.5), channel_id=1, source_target_pairs={{0,4},{4,8},{8,12},{12,16},{16,20},{20,24},{24,28},{28,32},{32,36}... | collective-permute-start | bytes 983048 | tf_op jit(solution)/shard_map/ppermute | solution.py:19
  242.5 1.9 copy.268
  244.4 8.7 %collective-permute-start.13 = (bf16[128,1280]{1,0:T(8,128)(2,1)}, bf16[128,1280]{1,0:T(8,128)(2,1)}, u32[]{:S(2)}, u32[]{:S(2)}) collective-permute-start(bf16[128,1280]{1,0:T(8,128)(2,1)} %collective-permute-done.12), channel_id=1, source_target_pairs={{0,4},{4,8},{8,12},{12,16},{16,20},{20,24},{24,28},{28,32},{32,36}... | collective-permute-start | bytes 983048 | tf_op jit(solution)/shard_map/ppermute | solution.py:19
  274.6 2.2 multiply_reduce_fusion.4
  281.4 1.9 collective-permute-start.21
  283.6 2.1 collective-permute-start.14
  286.2 190.9 %collective-permute-done.21 = f32[128,10,128]{2,0,1:T(8,128)S(1)} collective-permute-done((f32[128,10,128]{2,0,1:T(8,128)S(1)}, f32[128,10,128]{2,0,1:T(8,128)S(1)}, u32[]{:S(2)}, u32[]{:S(2)}) %collective-permute-start.21) | collective-permute-done | bytes 655392 | tf_op jit(solution)/shard_map/ppermute | solution.py:19
  477.5 1.9 collective-permute-start.22
  479.5 11.8 %collective-permute-done.14 = f32[128,10,128]{2,0,1:T(8,128)S(1)} collective-permute-done((f32[128,10,128]{2,0,1:T(8,128)S(1)}, f32[128,10,128]{2,0,1:T(8,128)S(1)}, u32[]{:S(2)}, u32[]{:S(2)}) %collective-permute-start.14) | collective-permute-done | bytes 655392 | tf_op jit(solution)/shard_map/ppermute | solution.py:19
  491.5 2.1 collective-permute-start.15
  495.2 10.1 %collective-permute-done.22 = f32[128,10,128]{2,0,1:T(8,128)S(1)} collective-permute-done((f32[128,10,128]{2,0,1:T(8,128)S(1)}, f32[128,10,128]{2,0,1:T(8,128)S(1)}, u32[]{:S(2)}, u32[]{:S(2)}) %collective-permute-start.22) | collective-permute-done | bytes 655392 | tf_op jit(solution)/shard_map/ppermute | solution.py:19
  505.4 1.9 collective-permute-start.23
  507.5 11.8 %collective-permute-done.15 = f32[128,10,128]{2,0,1:T(8,128)S(1)} collective-permute-done((f32[128,10,128]{2,0,1:T(8,128)S(1)}, f32[128,10,128]{2,0,1:T(8,128)S(1)}, u32[]{:S(2)}, u32[]{:S(2)}) %collective-permute-start.15) | collective-permute-done | bytes 655392 | tf_op jit(solution)/shard_map/ppermute | solution.py:19
  519.4 2.1 collective-permute-start.16
  522.0 11.3 %collective-permute-done.23 = f32[128,10,128]{2,0,1:T(8,128)S(1)} collective-permute-done((f32[128,10,128]{2,0,1:T(8,128)S(1)}, f32[128,10,128]{2,0,1:T(8,128)S(1)}, u32[]{:S(2)}, u32[]{:S(2)}) %collective-permute-start.23) | collective-permute-done | bytes 655392 | tf_op jit(solution)/shard_map/ppermute | solution.py:19
  533.4 1.9 collective-permute-start.24
  535.6 11.8 %collective-permute-done.16 = f32[128,10,128]{2,0,1:T(8,128)S(1)} collective-permute-done((f32[128,10,128]{2,0,1:T(8,128)S(1)}, f32[128,10,128]{2,0,1:T(8,128)S(1)}, u32[]{:S(2)}, u32[]{:S(2)}) %collective-permute-start.16) | collective-permute-done | bytes 655392 | tf_op jit(solution)/shard_map/ppermute | solution.py:19
  547.5 2.1 collective-permute-start.17
  550.3 11.2 %collective-permute-done.24 = f32[128,10,128]{2,0,1:T(8,128)S(1)} collective-permute-done((f32[128,10,128]{2,0,1:T(8,128)S(1)}, f32[128,10,128]{2,0,1:T(8,128)S(1)}, u32[]{:S(2)}, u32[]{:S(2)}) %collective-permute-start.24) | collective-permute-done | bytes 655392 | tf_op jit(solution)/shard_map/ppermute | solution.py:19
  561.5 1.9 collective-permute-start.25
  564.8 10.7 %collective-permute-done.17 = f32[128,10,128]{2,0,1:T(8,128)S(1)} collective-permute-done((f32[128,10,128]{2,0,1:T(8,128)S(1)}, f32[128,10,128]{2,0,1:T(8,128)S(1)}, u32[]{:S(2)}, u32[]{:S(2)}) %collective-permute-start.17) | collective-permute-done | bytes 655392 | tf_op jit(solution)/shard_map/ppermute | solution.py:19
  575.6 2.3 collective-permute-start.18
  578.6 11.0 %collective-permute-done.25 = f32[128,10,128]{2,0,1:T(8,128)S(1)} collective-permute-done((f32[128,10,128]{2,0,1:T(8,128)S(1)}, f32[128,10,128]{2,0,1:T(8,128)S(1)}, u32[]{:S(2)}, u32[]{:S(2)}) %collective-permute-start.25) | collective-permute-done | bytes 655392 | tf_op jit(solution)/shard_map/ppermute | solution.py:19
  589.6 1.9 collective-permute-start.26
  592.9 10.7 %collective-permute-done.18 = f32[128,10,128]{2,0,1:T(8,128)S(1)} collective-permute-done((f32[128,10,128]{2,0,1:T(8,128)S(1)}, f32[128,10,128]{2,0,1:T(8,128)S(1)}, u32[]{:S(2)}, u32[]{:S(2)}) %collective-permute-start.18) | collective-permute-done | bytes 655392 | tf_op jit(solution)/shard_map/ppermute | solution.py:19
  603.7 2.1 collective-permute-start.19
  608.5 9.2 %collective-permute-done.26 = f32[128,10,128]{2,0,1:T(8,128)S(1)} collective-permute-done((f32[128,10,128]{2,0,1:T(8,128)S(1)}, f32[128,10,128]{2,0,1:T(8,128)S(1)}, u32[]{:S(2)}, u32[]{:S(2)}) %collective-permute-start.26) | collective-permute-done | bytes 655392 | tf_op jit(solution)/shard_map/ppermute | solution.py:19
  618.5 1.9 collective-permute-start.27
  620.7 11.0 %collective-permute-done.19 = f32[128,10,128]{2,0,1:T(8,128)S(1)} collective-permute-done((f32[128,10,128]{2,0,1:T(8,128)S(1)}, f32[128,10,128]{2,0,1:T(8,128)S(1)}, u32[]{:S(2)}, u32[]{:S(2)}) %collective-permute-start.19) | collective-permute-done | bytes 655392 | tf_op jit(solution)/shard_map/ppermute | solution.py:19
  632.6 2.0 collective-permute-start.20
  638.2 10.8 %collective-permute-done.27 = f32[128,10,128]{2,0,1:T(8,128)} collective-permute-done((f32[128,10,128]{2,0,1:T(8,128)}, f32[128,10,128]{2,0,1:T(8,128)}, u32[]{:S(2)}, u32[]{:S(2)}) %collective-permute-start.27) | collective-permute-done | bytes 655392 | tf_op jit(solution)/shard_map/ppermute | solution.py:19
  651.0 11.9 %collective-permute-done.20 = f32[128,10,128]{2,0,1:T(8,128)} collective-permute-done((f32[128,10,128]{2,0,1:T(8,128)}, f32[128,10,128]{2,0,1:T(8,128)}, u32[]{:S(2)}, u32[]{:S(2)}) %collective-permute-start.20) | collective-permute-done | bytes 655392 | tf_op jit(solution)/shard_map/ppermute | solution.py:19
  664.5 5.9 all-reduce
  (293 shorter events, 92.7 us)
Async XLA Ops:
  2.8 30.0 %copy-start.19 = (bf16[1,128,1280]{1,2,0:T(8,128)(2,1)}, bf16[1,128,1280]{1,2,0:T(8,128)(2,1)S(1)}, u32[]{:S(2)}) copy-start(bf16[1,128,1280]{1,2,0:T(8,128)(2,1)S(1)} %copy.472) | copy-start | bytes 983044
  3.3 29.7 %copy-start.12 = (bf16[1,128,1280]{1,2,0:T(8,128)(2,1)}, bf16[1,128,1280]{1,2,0:T(8,128)(2,1)S(1)}, u32[]{:S(2)}) copy-start(bf16[1,128,1280]{1,2,0:T(8,128)(2,1)S(1)} %copy.473) | copy-start | bytes 983044
  4.9 134.4 %copy-start.14 = (bf16[1,128,1280]{1,2,0:T(8,128)(2,1)}, bf16[1,128,1280]{1,2,0:T(8,128)(2,1)S(1)}, u32[]{:S(2)}) copy-start(bf16[1,128,1280]{1,2,0:T(8,128)(2,1)S(1)} %copy.476) | copy-start | bytes 983044
  5.3 67.4 %copy-start.10 = (bf16[1,128,1280]{1,2,0:T(8,128)(2,1)}, bf16[1,128,1280]{1,2,0:T(8,128)(2,1)S(1)}, u32[]{:S(2)}) copy-start(bf16[1,128,1280]{1,2,0:T(8,128)(2,1)S(1)} %copy.475) | copy-start | bytes 983044
  12.9 18.8 %copy-start.65 = (bf16[128,1280]{1,0:T(8,128)(2,1)S(1)}, bf16[128,1280]{1,0:T(8,128)(2,1)}, u32[]{:S(2)}) copy-start(bf16[128,1280]{1,0:T(8,128)(2,1)} %param.7) | copy-start | bytes 983044
  13.8 17.8 %copy-start.39 = (bf16[128,1280]{0,1:T(8,128)(2,1)}, bf16[128,1280]{0,1:T(8,128)(2,1)S(1)}, u32[]{:S(2)}) copy-start(bf16[128,1280]{0,1:T(8,128)(2,1)S(1)} %get-tuple-element.48) | copy-start | bytes 983044
  13.8 62.6 %collective-permute-start = (bf16[128,1280]{0,1:T(8,128)(2,1)}, bf16[128,1280]{0,1:T(8,128)(2,1)}, u32[]{:S(2)}, u32[]{:S(2)}) collective-permute-start(bf16[128,1280]{0,1:T(8,128)(2,1)} %get-tuple-element.49), channel_id=1, source_target_pairs={{0,4},{4,8},{8,12},{12,16},{16,20},{20,24},{24,28},{28,32},{32,36}... | collective-permute-start | bytes 983048 | tf_op jit(solution)/shard_map/ppermute | solution.py:19
  19.2 65.8 %collective-permute-start.7 = (bf16[128,1280]{1,0:T(8,128)(2,1)}, bf16[128,1280]{1,0:T(8,128)(2,1)}, u32[]{:S(2)}, u32[]{:S(2)}) collective-permute-start(bf16[128,1280]{1,0:T(8,128)(2,1)} %get-tuple-element.40), channel_id=1, source_target_pairs={{0,4},{4,8},{8,12},{12,16},{16,20},{20,24},{24,28},{28,32},{32,36}... | collective-permute-start | bytes 983048 | tf_op jit(solution)/shard_map/ppermute | solution.py:19
  23.5 26.5 %collective-permute-start.29 = (bf16[64,1280]{0,1:T(8,128)(2,1)}, bf16[64,1280]{0,1:T(8,128)(2,1)}, u32[]{:S(2)}, u32[]{:S(2)}) collective-permute-start(bf16[64,1280]{0,1:T(8,128)(2,1)} %slice.87), channel_id=1, source_target_pairs={{0,4},{4,8},{8,12},{12,16},{16,20},{20,24},{24,28},{28,32},{32,36}... | collective-permute-start | bytes 491528 | tf_op jit(solution)/shard_map/ppermute | solution.py:19
  28.5 39.3 %collective-permute-start.28 = (bf16[64,1280]{1,0:T(8,128)(2,1)}, bf16[64,1280]{1,0:T(8,128)(2,1)S(1)}, u32[]{:S(2)}, u32[]{:S(2)}) collective-permute-start(bf16[64,1280]{1,0:T(8,128)(2,1)} %slice_bitcast_fusion), channel_id=1, source_target_pairs={{0,4},{4,8},{8,12},{12,16},{16,20},{20,24},{24,28},{28,32},{32,36}... | collective-permute-start | bytes 491528 | tf_op jit(solution)/shard_map/ppermute | solution.py:19
  33.0 4.7 copy-start.17
  33.2 4.7 copy-start.8
  37.9 12.1 %copy-start.40 = (bf16[128,1280]{0,1:T(8,128)(2,1)S(1)}, bf16[128,1280]{0,1:T(8,128)(2,1)}, u32[]{:S(2)}) copy-start(bf16[128,1280]{0,1:T(8,128)(2,1)} %copy-done.39) | copy-start | bytes 983044
  38.3 12.9 %copy-start.16 = (f32[128,10,128]{2,0,1:T(8,128)S(1)}, f32[128,10,128]{2,0,1:T(8,128)}, u32[]{:S(2)}) copy-start(f32[128,10,128]{2,0,1:T(8,128)} %copy.356) | copy-start | bytes 1966084
  51.7 16.1 %copy-start.41 = (bf16[128,10,128]{2,0,1:T(8,128)(2,1)S(1)}, bf16[128,10,128]{2,0,1:T(8,128)(2,1)}, u32[]{:S(2)}) copy-start(bf16[128,10,128]{2,0,1:T(8,128)(2,1)} %copy.354) | copy-start | bytes 983044
  69.8 4.1 copy-start.21
  70.8 51.6 %collective-permute-start.30 = (f32[64,10,128]{2,0,1:T(8,128)}, f32[64,10,128]{2,0,1:T(8,128)}, u32[]{:S(2)}, u32[]{:S(2)}) collective-permute-start(f32[64,10,128]{2,0,1:T(8,128)} %get-tuple-element.36), channel_id=1, source_target_pairs={{4,0},{8,4},{12,8},{16,12},{20,16},{24,20},{28,24},{32,28},{36,32}... | collective-permute-start | bytes 983048 | tf_op jit(solution)/shard_map/ppermute | solution.py:19
  76.1 13.0 %copy-start.48 = (f32[10,128,128]{1,2,0:T(8,128)S(1)}, f32[10,128,128]{1,2,0:T(8,128)}, u32[]{:S(2)}) copy-start(f32[10,128,128]{1,2,0:T(8,128)} %copy.362) | copy-start | bytes 1966084
  76.4 13.5 %copy-start.22 = (f32[192,10,128]{2,0,1:T(8,128)}, f32[192,10,128]{2,0,1:T(8,128)S(1)}, u32[]{:S(2)}) copy-start(f32[192,10,128]{2,0,1:T(8,128)S(1)} %convolution_bitcast_fusion) | copy-start | bytes 2949124
  76.4 13.5 %copy-start.36 = (f32[64,10,128]{2,0,1:T(8,128)S(1)}, f32[64,10,128]{2,0,1:T(8,128)}, u32[]{:S(2)}) copy-start(f32[64,10,128]{2,0,1:T(8,128)} %get-tuple-element.35) | copy-start | bytes 983044
  76.4 31.0 %collective-permute-start.1 = (bf16[128,1280]{0,1:T(8,128)(2,1)}, bf16[128,1280]{0,1:T(8,128)(2,1)}, u32[]{:S(2)}, u32[]{:S(2)}) collective-permute-start(bf16[128,1280]{0,1:T(8,128)(2,1)} %collective-permute-done), channel_id=1, source_target_pairs={{0,4},{4,8},{8,12},{12,16},{16,20},{20,24},{24,28},{28,32},{32,36}... | collective-permute-start | bytes 983048 | tf_op jit(solution)/shard_map/ppermute | solution.py:19
  85.1 31.0 %collective-permute-start.8 = (bf16[128,1280]{1,0:T(8,128)(2,1)}, bf16[128,1280]{1,0:T(8,128)(2,1)}, u32[]{:S(2)}, u32[]{:S(2)}) collective-permute-start(bf16[128,1280]{1,0:T(8,128)(2,1)} %collective-permute-done.7), channel_id=1, source_target_pairs={{0,4},{4,8},{8,12},{12,16},{16,20},{20,24},{24,28},{28,32},{32,36}... | collective-permute-start | bytes 983048 | tf_op jit(solution)/shard_map/ppermute | solution.py:19
  93.0 55.9 %collective-permute-start.31 = (f32[64,10,128]{2,0,1:T(8,128)}, f32[64,10,128]{2,0,1:T(8,128)}, u32[]{:S(2)}, u32[]{:S(2)}) collective-permute-start(f32[64,10,128]{2,0,1:T(8,128)} %slice.93), channel_id=1, source_target_pairs={{4,0},{8,4},{12,8},{16,12},{20,16},{24,20},{28,24},{32,28},{36,32}... | collective-permute-start | bytes 983048 | tf_op jit(solution)/shard_map/ppermute | solution.py:19
  107.4 23.3 %collective-permute-start.2 = (bf16[128,1280]{0,1:T(8,128)(2,1)}, bf16[128,1280]{0,1:T(8,128)(2,1)S(1)}, u32[]{:S(2)}, u32[]{:S(2)}) collective-permute-start(bf16[128,1280]{0,1:T(8,128)(2,1)} %collective-permute-done.1), channel_id=1, source_target_pairs={{0,4},{4,8},{8,12},{12,16},{16,20},{20,24},{24,28},{28,32},{32,36}... | collective-permute-start | bytes 983048 | tf_op jit(solution)/shard_map/ppermute | solution.py:19
  116.1 24.8 %collective-permute-start.9 = (bf16[128,1280]{1,0:T(8,128)(2,1)}, bf16[128,1280]{1,0:T(8,128)(2,1)}, u32[]{:S(2)}, u32[]{:S(2)}) collective-permute-start(bf16[128,1280]{1,0:T(8,128)(2,1)} %collective-permute-done.8), channel_id=1, source_target_pairs={{0,4},{4,8},{8,12},{12,16},{16,20},{20,24},{24,28},{28,32},{32,36}... | collective-permute-start | bytes 983048 | tf_op jit(solution)/shard_map/ppermute | solution.py:19
  125.5 13.8 %copy-start.47 = (f32[64,10,128]{0,2,1:T(8,128)S(1)}, f32[64,10,128]{0,2,1:T(8,128)}, u32[]{:S(2)}) copy-start(f32[64,10,128]{0,2,1:T(8,128)} %copy.468) | copy-start | bytes 983044
  130.8 53.9 %copy-start.54 = (bf16[128,1280]{0,1:T(8,128)(2,1)}, bf16[128,1280]{0,1:T(8,128)(2,1)S(1)}, u32[]{:S(2)}) copy-start(bf16[128,1280]{0,1:T(8,128)(2,1)S(1)} %collective-permute-done.2) | copy-start | bytes 983044
  130.8 21.6 %collective-permute-start.3 = (bf16[128,1280]{0,1:T(8,128)(2,1)S(1)}, bf16[128,1280]{0,1:T(8,128)(2,1)}, u32[]{:S(2)}, u32[]{:S(2)}) collective-permute-start(bf16[128,1280]{0,1:T(8,128)(2,1)S(1)} %collective-permute-done.2), channel_id=1, source_target_pairs={{0,4},{4,8},{8,12},{12,16},{16,20},{20,24},{24,28},{28,32},{32,36}... | collective-permute-start | bytes 983048 | tf_op jit(solution)/shard_map/ppermute | solution.py:19
  140.9 22.2 %collective-permute-start.10 = (bf16[128,1280]{1,0:T(8,128)(2,1)}, bf16[128,1280]{1,0:T(8,128)(2,1)}, u32[]{:S(2)}, u32[]{:S(2)}) collective-permute-start(bf16[128,1280]{1,0:T(8,128)(2,1)} %collective-permute-done.9), channel_id=1, source_target_pairs={{0,4},{4,8},{8,12},{12,16},{16,20},{20,24},{24,28},{28,32},{32,36}... | collective-permute-start | bytes 983048 | tf_op jit(solution)/shard_map/ppermute | solution.py:19
  152.3 23.7 %collective-permute-start.4 = (bf16[128,1280]{0,1:T(8,128)(2,1)}, bf16[128,1280]{0,1:T(8,128)(2,1)S(1)}, u32[]{:S(2)}, u32[]{:S(2)}) collective-permute-start(bf16[128,1280]{0,1:T(8,128)(2,1)} %collective-permute-done.3), channel_id=1, source_target_pairs={{0,4},{4,8},{8,12},{12,16},{16,20},{20,24},{24,28},{28,32},{32,36}... | collective-permute-start | bytes 983048 | tf_op jit(solution)/shard_map/ppermute | solution.py:19
  163.1 39.9 %collective-permute-start.11 = (bf16[128,1280]{1,0:T(8,128)(2,1)}, bf16[128,1280]{1,0:T(8,128)(2,1)}, u32[]{:S(2)}, u32[]{:S(2)}) collective-permute-start(bf16[128,1280]{1,0:T(8,128)(2,1)} %collective-permute-done.10), channel_id=1, source_target_pairs={{0,4},{4,8},{8,12},{12,16},{16,20},{20,24},{24,28},{28,32},{32,36}... | collective-permute-start | bytes 983048 | tf_op jit(solution)/shard_map/ppermute | solution.py:19
  176.1 61.8 %copy-start.56 = (bf16[128,1280]{0,1:T(8,128)(2,1)}, bf16[128,1280]{0,1:T(8,128)(2,1)S(1)}, u32[]{:S(2)}) copy-start(bf16[128,1280]{0,1:T(8,128)(2,1)S(1)} %collective-permute-done.4) | copy-start | bytes 983044
  176.1 49.2 %collective-permute-start.5 = (bf16[128,1280]{0,1:T(8,128)(2,1)S(1)}, bf16[128,1280]{0,1:T(8,128)(2,1)}, u32[]{:S(2)}, u32[]{:S(2)}) collective-permute-start(bf16[128,1280]{0,1:T(8,128)(2,1)S(1)} %collective-permute-done.4), channel_id=1, source_target_pairs={{0,4},{4,8},{8,12},{12,16},{16,20},{20,24},{24,28},{28,32},{32,36}... | collective-permute-start | bytes 983048 | tf_op jit(solution)/shard_map/ppermute | solution.py:19
  203.0 39.4 %collective-permute-start.12 = (bf16[128,1280]{1,0:T(8,128)(2,1)}, bf16[128,1280]{1,0:T(8,128)(2,1)}, u32[]{:S(2)}, u32[]{:S(2)}) collective-permute-start(bf16[128,1280]{1,0:T(8,128)(2,1)} %collective-permute-done.11), channel_id=1, source_target_pairs={{0,4},{4,8},{8,12},{12,16},{16,20},{20,24},{24,28},{28,32},{32,36}... | collective-permute-start | bytes 983048 | tf_op jit(solution)/shard_map/ppermute | solution.py:19
  225.2 29.1 %collective-permute-start.6 = (bf16[128,1280]{0,1:T(8,128)(2,1)}, bf16[128,1280]{0,1:T(8,128)(2,1)S(1)}, u32[]{:S(2)}, u32[]{:S(2)}) collective-permute-start(bf16[128,1280]{0,1:T(8,128)(2,1)} %collective-permute-done.5), channel_id=1, source_target_pairs={{0,4},{4,8},{8,12},{12,16},{16,20},{20,24},{24,28},{28,32},{32,36}... | collective-permute-start | bytes 983048 | tf_op jit(solution)/shard_map/ppermute | solution.py:19
  244.4 28.3 %collective-permute-start.13 = (bf16[128,1280]{1,0:T(8,128)(2,1)}, bf16[128,1280]{1,0:T(8,128)(2,1)}, u32[]{:S(2)}, u32[]{:S(2)}) collective-permute-start(bf16[128,1280]{1,0:T(8,128)(2,1)} %collective-permute-done.12), channel_id=1, source_target_pairs={{0,4},{4,8},{8,12},{12,16},{16,20},{20,24},{24,28},{28,32},{32,36}... | collective-permute-start | bytes 983048 | tf_op jit(solution)/shard_map/ppermute | solution.py:19
  254.4 17.1 %copy-start.6 = (f32[10,128,128]{1,2,0:T(8,128)}, f32[10,128,128]{1,2,0:T(8,128)S(1)}, u32[]{:S(2)}) copy-start(f32[10,128,128]{1,2,0:T(8,128)S(1)} %get-tuple-element.62) | copy-start | bytes 1966084
  281.4 195.8 %collective-permute-start.21 = (f32[128,10,128]{2,0,1:T(8,128)S(1)}, f32[128,10,128]{2,0,1:T(8,128)S(1)}, u32[]{:S(2)}, u32[]{:S(2)}) collective-permute-start(f32[128,10,128]{2,0,1:T(8,128)S(1)} %copy-done.64), channel_id=1, source_target_pairs={{4,0},{8,4},{12,8},{16,12},{20,16},{24,20},{28,24},{32,28},{36,32}... | collective-permute-start | bytes 1966088 | tf_op jit(solution)/shard_map/ppermute | solution.py:19
  283.6 207.6 %collective-permute-start.14 = (f32[128,10,128]{2,0,1:T(8,128)S(1)}, f32[128,10,128]{2,0,1:T(8,128)S(1)}, u32[]{:S(2)}, u32[]{:S(2)}) collective-permute-start(f32[128,10,128]{2,0,1:T(8,128)S(1)} %fusion.12), channel_id=1, source_target_pairs={{4,0},{8,4},{12,8},{16,12},{20,16},{24,20},{28,24},{32,28},{36,32}... | collective-permute-start | bytes 1966088 | tf_op jit(solution)/shard_map/ppermute | solution.py:19
  477.5 27.7 %collective-permute-start.22 = (f32[128,10,128]{2,0,1:T(8,128)S(1)}, f32[128,10,128]{2,0,1:T(8,128)S(1)}, u32[]{:S(2)}, u32[]{:S(2)}) collective-permute-start(f32[128,10,128]{2,0,1:T(8,128)S(1)} %fusion.13), channel_id=1, source_target_pairs={{4,0},{8,4},{12,8},{16,12},{20,16},{24,20},{28,24},{32,28},{36,32}... | collective-permute-start | bytes 1966088 | tf_op jit(solution)/shard_map/ppermute | solution.py:19
  491.5 27.8 %collective-permute-start.15 = (f32[128,10,128]{2,0,1:T(8,128)S(1)}, f32[128,10,128]{2,0,1:T(8,128)S(1)}, u32[]{:S(2)}, u32[]{:S(2)}) collective-permute-start(f32[128,10,128]{2,0,1:T(8,128)S(1)} %fusion.38), channel_id=1, source_target_pairs={{4,0},{8,4},{12,8},{16,12},{20,16},{24,20},{28,24},{32,28},{36,32}... | collective-permute-start | bytes 1966088 | tf_op jit(solution)/shard_map/ppermute | solution.py:19
  494.9 10.4 %copy-start.46 = (f32[128,10,128]{2,0,1:T(8,128)S(1)}, f32[128,10,128]{2,0,1:T(8,128)}, u32[]{:S(2)}) copy-start(f32[128,10,128]{2,0,1:T(8,128)} %convolution_bitcast_fusion.6) | copy-start | bytes 1966084
  505.4 28.0 %collective-permute-start.23 = (f32[128,10,128]{2,0,1:T(8,128)S(1)}, f32[128,10,128]{2,0,1:T(8,128)S(1)}, u32[]{:S(2)}, u32[]{:S(2)}) collective-permute-start(f32[128,10,128]{2,0,1:T(8,128)S(1)} %add.274), channel_id=1, source_target_pairs={{4,0},{8,4},{12,8},{16,12},{20,16},{24,20},{28,24},{32,28},{36,32}... | collective-permute-start | bytes 1966088 | tf_op jit(solution)/shard_map/ppermute | solution.py:19
  519.4 28.0 %collective-permute-start.16 = (f32[128,10,128]{2,0,1:T(8,128)S(1)}, f32[128,10,128]{2,0,1:T(8,128)S(1)}, u32[]{:S(2)}, u32[]{:S(2)}) collective-permute-start(f32[128,10,128]{2,0,1:T(8,128)S(1)} %add.267), channel_id=1, source_target_pairs={{4,0},{8,4},{12,8},{16,12},{20,16},{24,20},{28,24},{32,28},{36,32}... | collective-permute-start | bytes 1966088 | tf_op jit(solution)/shard_map/ppermute | solution.py:19
  521.7 11.6 %copy-start.45 = (f32[128,10,128]{2,0,1:T(8,128)S(1)}, f32[128,10,128]{2,0,1:T(8,128)}, u32[]{:S(2)}) copy-start(f32[128,10,128]{2,0,1:T(8,128)} %convolution_bitcast_fusion.5) | copy-start | bytes 1966084
  533.4 28.0 %collective-permute-start.24 = (f32[128,10,128]{2,0,1:T(8,128)S(1)}, f32[128,10,128]{2,0,1:T(8,128)S(1)}, u32[]{:S(2)}, u32[]{:S(2)}) collective-permute-start(f32[128,10,128]{2,0,1:T(8,128)S(1)} %add.275), channel_id=1, source_target_pairs={{4,0},{8,4},{12,8},{16,12},{20,16},{24,20},{28,24},{32,28},{36,32}... | collective-permute-start | bytes 1966088 | tf_op jit(solution)/shard_map/ppermute | solution.py:19
  535.6 13.9 %copy-start.55 = (bf16[128,1280]{0,1:T(8,128)(2,1)S(1)}, bf16[128,1280]{0,1:T(8,128)(2,1)}, u32[]{:S(2)}) copy-start(bf16[128,1280]{0,1:T(8,128)(2,1)} %copy-done.54) | copy-start | bytes 983044
  547.5 28.0 %collective-permute-start.17 = (f32[128,10,128]{2,0,1:T(8,128)S(1)}, f32[128,10,128]{2,0,1:T(8,128)S(1)}, u32[]{:S(2)}, u32[]{:S(2)}) collective-permute-start(f32[128,10,128]{2,0,1:T(8,128)S(1)} %add.268), channel_id=1, source_target_pairs={{4,0},{8,4},{12,8},{16,12},{20,16},{24,20},{28,24},{32,28},{36,32}... | collective-permute-start | bytes 1966088 | tf_op jit(solution)/shard_map/ppermute | solution.py:19
  549.9 11.5 %copy-start.44 = (f32[128,10,128]{2,0,1:T(8,128)S(1)}, f32[128,10,128]{2,0,1:T(8,128)}, u32[]{:S(2)}) copy-start(f32[128,10,128]{2,0,1:T(8,128)} %convolution_bitcast_fusion.4) | copy-start | bytes 1966084
  561.5 28.0 %collective-permute-start.25 = (f32[128,10,128]{2,0,1:T(8,128)S(1)}, f32[128,10,128]{2,0,1:T(8,128)S(1)}, u32[]{:S(2)}, u32[]{:S(2)}) collective-permute-start(f32[128,10,128]{2,0,1:T(8,128)S(1)} %add.276), channel_id=1, source_target_pairs={{4,0},{8,4},{12,8},{16,12},{20,16},{24,20},{28,24},{32,28},{36,32}... | collective-permute-start | bytes 1966088 | tf_op jit(solution)/shard_map/ppermute | solution.py:19
  564.8 13.1 %copy-start.57 = (bf16[128,1280]{0,1:T(8,128)(2,1)S(1)}, bf16[128,1280]{0,1:T(8,128)(2,1)}, u32[]{:S(2)}) copy-start(bf16[128,1280]{0,1:T(8,128)(2,1)} %copy-done.56) | copy-start | bytes 983044
  575.6 28.0 %collective-permute-start.18 = (f32[128,10,128]{2,0,1:T(8,128)S(1)}, f32[128,10,128]{2,0,1:T(8,128)S(1)}, u32[]{:S(2)}, u32[]{:S(2)}) collective-permute-start(f32[128,10,128]{2,0,1:T(8,128)S(1)} %add.269), channel_id=1, source_target_pairs={{4,0},{8,4},{12,8},{16,12},{20,16},{24,20},{28,24},{32,28},{36,32}... | collective-permute-start | bytes 1966088 | tf_op jit(solution)/shard_map/ppermute | solution.py:19
  578.2 11.3 %copy-start.43 = (f32[128,10,128]{2,0,1:T(8,128)S(1)}, f32[128,10,128]{2,0,1:T(8,128)}, u32[]{:S(2)}) copy-start(f32[128,10,128]{2,0,1:T(8,128)} %convolution_bitcast_fusion.3) | copy-start | bytes 1966084
  589.6 28.0 %collective-permute-start.26 = (f32[128,10,128]{2,0,1:T(8,128)S(1)}, f32[128,10,128]{2,0,1:T(8,128)S(1)}, u32[]{:S(2)}, u32[]{:S(2)}) collective-permute-start(f32[128,10,128]{2,0,1:T(8,128)S(1)} %add.277), channel_id=1, source_target_pairs={{4,0},{8,4},{12,8},{16,12},{20,16},{24,20},{28,24},{32,28},{36,32}... | collective-permute-start | bytes 1966088 | tf_op jit(solution)/shard_map/ppermute | solution.py:19
  603.6 3.4 copy-start.18
  603.7 3.4 copy-start.63
  603.7 28.0 %collective-permute-start.19 = (f32[128,10,128]{2,0,1:T(8,128)S(1)}, f32[128,10,128]{2,0,1:T(8,128)S(1)}, u32[]{:S(2)}, u32[]{:S(2)}) collective-permute-start(f32[128,10,128]{2,0,1:T(8,128)S(1)} %add.270), channel_id=1, source_target_pairs={{4,0},{8,4},{12,8},{16,12},{20,16},{24,20},{28,24},{32,28},{36,32}... | collective-permute-start | bytes 1966088 | tf_op jit(solution)/shard_map/ppermute | solution.py:19
  607.1 10.5 %copy-start.42 = (f32[128,10,128]{2,0,1:T(8,128)S(1)}, f32[128,10,128]{2,0,1:T(8,128)}, u32[]{:S(2)}) copy-start(f32[128,10,128]{2,0,1:T(8,128)} %convolution_bitcast_fusion.2) | copy-start | bytes 1966084
  618.5 30.4 %collective-permute-start.27 = (f32[128,10,128]{2,0,1:T(8,128)}, f32[128,10,128]{2,0,1:T(8,128)}, u32[]{:S(2)}, u32[]{:S(2)}) collective-permute-start(f32[128,10,128]{2,0,1:T(8,128)} %add.278), channel_id=1, source_target_pairs={{4,0},{8,4},{12,8},{16,12},{20,16},{24,20},{28,24},{32,28},{36,32}... | collective-permute-start | bytes 1966088 | tf_op jit(solution)/shard_map/ppermute | solution.py:19
  632.6 4.2 copy-start.52
  632.6 30.3 %collective-permute-start.20 = (f32[128,10,128]{2,0,1:T(8,128)}, f32[128,10,128]{2,0,1:T(8,128)}, u32[]{:S(2)}, u32[]{:S(2)}) collective-permute-start(f32[128,10,128]{2,0,1:T(8,128)} %add.271), channel_id=1, source_target_pairs={{4,0},{8,4},{12,8},{16,12},{20,16},{24,20},{28,24},{32,28},{36,32}... | collective-permute-start | bytes 1966088 | tf_op jit(solution)/shard_map/ppermute | solution.py:19
  664.2 6.2 copy-start.13
  664.2 6.2 copy-start.15
  664.2 6.2 copy-start.50
  (37 other events, 56.6 us)
where the time goes:
time: 678 us; the launch traced here: 676 us
  waiting for transfers between devices  404 us (60%)
  starting transfers between devices  147 us (22%)
  local copies, waits for them, and re-layouts  54 us (8%)
  matrix products  39.2 us (6%)
  other arithmetic  15.7 us (2%)
  blocking collectives  13.2 us (2%)
    ppermute x32, waiting for transfers between devices, passed_along(): return lax.ppermute(shard, axis, pairs)  404 us
    ppermute x32, starting transfers between devices, passed_along(): return lax.ppermute(shard, axis, pairs)  147 us
    unnamed x149, local copies, waits for them, and re-layouts  19.4 us
  transfers between devices with their start and end apart: 32, of which 23 were waited for; matrix products, arithmetic and copies ran while one was open for 12% of the time, Pallas kernels for 0%

commit v1 on v0

v1 whole, which is shorter than its diff:
```python
import jax
import jax.numpy as jnp
from jax import lax
from jax.experimental import pallas as pl
from jax.experimental.pallas import tpu as pltpu
from jax.sharding import PartitionSpec as P

MESH = pl.DeviceIdType.MESH
BF16 = jnp.bfloat16
F32 = jnp.float32
HEAD_DIM = 128
WIDTH = 5120
DOC_MAX = 64
ROWS = 128
LOCAL = 1280
HEADS = 10
HALF = 512
EPSILON = 1e-06
NEGATIVE = -1e30
FACTOR = HEAD_DIM ** (-0.5)


def first_head(x, core):
    return lax.div(5 * x + 1 - core, 2)


def has_third(x, core):
    return lax.rem(x + core, 2) == 0


def columns(head):
    return pl.ds(pl.multiple_of(head * HEAD_DIM, HEAD_DIM), HEAD_DIM)


def block_rows(x):
    return pl.ds(pl.multiple_of(x * ROWS, ROWS), ROWS)


def await_bytes(ref, sem):
    pltpu.make_async_copy(ref, ref, sem).wait()


def dot(a, b):
    return jnp.dot(a, b, preferred_element_type=F32)


def dot_t(a, b):
    return lax.dot_general(a, b, (((1,), (1,)), ((), ())), preferred_element_type=F32)


def attend(q, do, pieces):
    scores = []
    for k, v, mask in pieces:
        s = dot_t(k, q) * FACTOR
        scores.append(s if mask is None else jnp.where(mask, s, NEGATIVE))
    high = jnp.max(scores[0], axis=0, keepdims=True)
    for s in scores[1:]:
        high = jnp.maximum(high, jnp.max(s, axis=0, keepdims=True))
    powers = [jnp.exp(s - high) for s in scores]
    total = jnp.sum(powers[0], axis=0, keepdims=True)
    for p in powers[1:]:
        total = total + jnp.sum(p, axis=0, keepdims=True)
    log_total = high + jnp.log(total)
    share = 1.0 / total
    probs = [p * share for p in powers]
    weights = [p.astype(BF16) for p in probs]
    out_t = dot(pieces[0][1].T, weights[0])
    for (k, v, mask), w in zip(pieces[1:], weights[1:]):
        out_t = out_t + dot(v.T, w)
    out = out_t.T.astype(BF16)
    row_dot = jnp.sum(do.astype(F32).T * out_t.astype(BF16).astype(F32), axis=0, keepdims=True)
    grads = [
        (p * (dot_t(v, do) - row_dot)).astype(BF16) for (k, v, mask), p in zip(pieces, probs)
    ]
    dq_t = dot(pieces[0][0].T, grads[0])
    for (k, v, mask), g in zip(pieces[1:], grads[1:]):
        dq_t = dq_t + dot(k.T, g)
    return out, (dq_t * FACTOR).T, log_total, row_dot, weights, grads


def to_rows(cols):
    lane = lax.broadcasted_iota(jnp.int32, (ROWS, HEAD_DIM), 1)
    packed = jnp.zeros((ROWS, HEAD_DIM), F32)
    for i, col in enumerate(cols):
        packed = jnp.where(lane == i, col, packed)
    return packed.T[:8]


def to_cols(rows):
    return jnp.concatenate([rows] * (ROWS // 8), axis=0).T


def kernel(
    lqkv, lgrad, sqkv, sgrad, lengths, gains,
    lout, ldqkv, sout, sdqkv,
    raw, nlong, sq, kx, vx, sdo, inv, sums, sums_in,
    t, z, stats, stats_in, g, acc, r, so, sd, rim_out, rim_in, fin,
    load, v_s, v_r, q_s, q_r, z_s, z_r, l_s, l_r, b_s, b_r, h_s, h_r, m_s, m_r, o_s,
):
    c = lax.axis_index("ctx")
    h = lax.axis_index("head")
    x = lax.rem(c, 4)
    row_base = c - x
    par = lax.rem(lax.div(c, 4), 2)
    core = lax.rem(h, 2)
    third = has_third(x, core)
    count = jnp.where(third, 3, 2)
    first = first_head(x, core)
    mate = (c + 4 - 8 * par, h)
    after = (lax.rem(c + 1, 64), h)
    before = (lax.rem(c + 63, 64), h)

    def x_at(d):
        return lax.rem(x + d, 4)

    def x_dev(d):
        return (row_base + x_at(d), h)

    def head_dev(d):
        return (c, lax.rem(h + d, 4))

    def remote(src, dst, send, recv, dev):
        return pltpu.make_async_remote_copy(
            src_ref=src, dst_ref=dst, send_sem=send, recv_sem=recv,
            device_id=dev, device_id_type=MESH,
        )

    loads = [
        pltpu.make_async_copy(lqkv.at[0], raw.at[0], load.at[0]),
        pltpu.make_async_copy(lqkv.at[1], raw.at[1], load.at[1]),
        pltpu.make_async_copy(sqkv.at[0], raw.at[2], load.at[2]),
        pltpu.make_async_copy(sqkv.at[1], raw.at[3], load.at[3]),
        pltpu.make_async_copy(sqkv.at[2], vx.at[pl.ds(DOC_MAX, ROWS)], load.at[4]),
        pltpu.make_async_copy(sgrad, sdo, load.at[5]),
    ]
    for copy in loads:
        copy.start()

    peers = [x_dev(1), x_dev(2), x_dev(3), mate, head_dev(1), head_dev(2), head_dev(3), after, before]
    barrier = pltpu.get_barrier_semaphore()
    for dev in peers:
        pl.semaphore_signal(barrier, inc=1, device_id=dev, device_id_type=MESH)

    mine = block_rows(x)

    def own_values(s):
        for kind, src in ((0, lqkv.at[2]), (1, lgrad)):
            pltpu.make_async_copy(
                src.at[:, columns(first + s)], t.at[s, 2 + kind, mine], v_r.at[kind, s, 0]
            ).start()

    def send_values(s, d):
        for kind, src in ((0, lqkv.at[2]), (1, lgrad)):
            remote(
                src.at[:, columns(first_head(x_at(d), core) + s)], t.at[s, 2 + kind, mine],
                v_s.at[kind, s, d], v_r.at[kind, s, d], x_dev(d),
            ).start()

    def send_keys(s, d):
        remote(
            nlong.at[:, :, columns(first_head(x_at(d), core) + s)], t.at[s, pl.ds(0, 2), mine],
            q_s.at[s, d], q_r.at[s, d], x_dev(d),
        ).start()

    def own_keys(s):
        pltpu.make_async_copy(
            nlong.at[:, :, columns(first + s)], t.at[s, pl.ds(0, 2), mine], q_r.at[s, 0]
        ).start()

    def to_peers(s, send):
        for d in (1, 2, 3):
            if s < 2:
                send(s, d)
            else:
                pl.when(has_third(x_at(d), core))(lambda d=d: send(s, d))

    own_values(0)
    own_values(1)
    pl.when(third)(lambda: own_values(2))

    pl.semaphore_wait(barrier, len(peers))

    to_peers(0, send_values)
    rim_v = remote(
        sqkv.at[2, pl.ds(ROWS - DOC_MAX, DOC_MAX)], vx.at[pl.ds(0, DOC_MAX)],
        m_s.at[0], m_r.at[0], after,
    )
    rim_v.start()

    for copy in loads[:4]:
        copy.wait()

    def square_step(j, sums_so_far):
        cols = columns(j)
        new = []
        for i in range(4):
            w = raw[i, :, cols].astype(F32)
            new.append(sums_so_far[i] + w * w)
        return tuple(new)

    zero = jnp.zeros((ROWS, HEAD_DIM), F32)
    squares = lax.fori_loop(0, HEADS, square_step, (zero,) * 4)
    sums[0] = to_rows([jnp.sum(a, axis=1, keepdims=True) for a in squares])
    for d in (1, 2, 3):
        remote(sums.at[0], sums_in.at[0, d], h_s.at[0, d], h_r.at[0, d], head_dev(d)).start()
    for d in (1, 2, 3):
        await_bytes(sums_in.at[0, d], h_r.at[0, d])
    all_sums = sums[0] + sums_in[0, 1] + sums_in[0, 2] + sums_in[0, 3]
    inv[...] = to_cols(lax.rsqrt(all_sums / WIDTH + EPSILON))

    def normalize_step(j, _):
        cols = columns(j)
        nlong[0, :, cols] = (raw[0, :, cols].astype(F32) * inv[:, 0:1] * gains[0:1, cols]).astype(BF16)
        nlong[1, :, cols] = (raw[1, :, cols].astype(F32) * inv[:, 1:2] * gains[1:2, cols]).astype(BF16)
        sq[:, cols] = (raw[2, :, cols].astype(F32) * inv[:, 2:3] * gains[0:1, cols]).astype(BF16)
        kx[pl.ds(DOC_MAX, ROWS), cols] = (
            raw[3, :, cols].astype(F32) * inv[:, 3:4] * gains[1:2, cols]
        ).astype(BF16)
        return 0

    lax.fori_loop(0, HEADS, normalize_step, 0)

    own_keys(0)
    own_keys(1)
    pl.when(third)(lambda: own_keys(2))
    to_peers(0, send_keys)
    to_peers(1, send_values)
    to_peers(1, send_keys)
    remote(
        kx.at[pl.ds(ROWS, DOC_MAX)], kx.at[pl.ds(0, DOC_MAX)], m_s.at[1], m_r.at[1], after
    ).start()
    to_peers(2, send_values)
    to_peers(2, send_keys)

    diag = lax.broadcasted_iota(jnp.int32, (256, 256), 0) <= lax.broadcasted_iota(
        jnp.int32, (256, 256), 1
    )

    def send_back(s, pair):
        for d in (1, 2, 3):
            remote(
                g.at[s, pl.ds(2 * pair, 2), block_rows(x_at(d))],
                r.at[pl.ds(2 * pair, 2), :, columns(first + s)],
                b_s.at[pair, s, d], b_r.at[pair, s, d], x_dev(d),
            ).start()
        pltpu.make_async_copy(
            g.at[s, pl.ds(2 * pair, 2), mine], r.at[pl.ds(2 * pair, 2), :, columns(first + s)],
            b_r.at[pair, s, 0],
        ).start()

    def relay(s):
        for d in range(4):
            rows = block_rows(lax.rem(x + 4 - d, 4))
            await_bytes(t.at[s, 2, rows], v_r.at[0, s, d])
            await_bytes(t.at[s, 3, rows], v_r.at[1, s, d])
            remote(t.at[s, 2 + par, rows], z.at[s, 0, rows], z_s.at[0, s, d], z_r.at[0, s, d], mate).start()
        for d in range(4):
            rows = block_rows(lax.rem(x + 4 - d, 4))
            await_bytes(t.at[s, pl.ds(0, 2), rows], q_r.at[s, d])
            remote(t.at[s, 1 - par, rows], z.at[s, 1, rows], z_s.at[1, s, d], z_r.at[1, s, d], mate).start()

    def within(s, i, early, keep):
        rows = pl.ds(i * 256, 256)
        q, do = t[s, 0, rows], t[s, 3, rows]
        pieces = list(early)
        if i:
            pieces.append((t[s, 1, pl.ds(0, 256)], t[s, 2, pl.ds(0, 256)], None))
        pieces.append((t[s, 1, rows], t[s, 2, rows], diag))
        out, dq, log_total, row_dot, weights, grads = attend(q, do, pieces)
        g[s, 0, rows] = out
        g[s, 1, rows] = dq.astype(BF16)
        if keep:
            stats[s, 0:1, rows] = log_total
            stats[s, 1:2, rows] = row_dot
        base = len(early)
        if i:
            acc[s, 0, pl.ds(0, 256)] = acc[s, 0, pl.ds(0, 256)] + dot(grads[base], q)
            acc[s, 1, pl.ds(0, 256)] = acc[s, 1, pl.ds(0, 256)] + dot(weights[base], do)
        acc[s, 0, rows] = dot(grads[-1], q)
        acc[s, 1, rows] = dot(weights[-1], do)

    def first_half(s):
        for i in range(2):
            within(s, i, [], False)
        send_back(s, 0)

    def relay_step(s, _):
        relay(s)
        pl.when(par == 0)(lambda: first_half(s))
        return 0

    lax.fori_loop(0, count, relay_step, 0)

    for copy in loads[4:]:
        copy.wait()
    await_bytes(vx.at[pl.ds(0, DOC_MAX)], m_r.at[0])
    await_bytes(kx.at[pl.ds(0, DOC_MAX)], m_r.at[1])
    docs = lengths.shape[1]
    until = lax.broadcasted_iota(jnp.int32, (docs, docs), 1) <= lax.broadcasted_iota(
        jnp.int32, (docs, docs), 0
    )
    ends = jnp.sum(jnp.where(until, lengths[...], 0), axis=1, keepdims=True)
    query_pos = c * ROWS + lax.broadcasted_iota(jnp.int32, (1, ROWS), 1)
    begin = jnp.max(jnp.where(ends <= query_pos, ends, 0), axis=0, keepdims=True)
    key_pos = c * ROWS - DOC_MAX + lax.broadcasted_iota(jnp.int32, (ROWS + DOC_MAX, ROWS), 0)
    allowed = (key_pos <= query_pos) & (key_pos >= begin)

    def short_step(j, _):
        cols = columns(j)
        q, do = sq[:, cols], sdo[:, cols]
        out, dq, _, _, weights, grads = attend(q, do, [(kx[:, cols], vx[:, cols], allowed)])
        so[:, cols] = out
        sd[0, :, cols] = dq
        dk = dot(grads[0], q) * FACTOR
        dv = dot(weights[0], do)
        sd[1, :, cols] = dk[DOC_MAX:]
        sd[2, :, cols] = dv[DOC_MAX:]
        rim_out[0, :, cols] = dk[:DOC_MAX].astype(BF16)
        rim_out[1, :, cols] = dv[:DOC_MAX].astype(BF16)
        return 0

    lax.fori_loop(0, HEADS, short_step, 0)
    remote(rim_out, rim_in, m_s.at[2], m_r.at[2], before).start()
    pltpu.make_async_copy(so, sout, o_s.at[0]).start()

    def await_mate(s):
        for d in range(4):
            rows = block_rows(lax.rem(x + 4 - d, 4))
            await_bytes(z.at[s, 0, rows], z_r.at[0, s, d])
            await_bytes(z.at[s, 1, rows], z_r.at[1, s, d])

    def put_key_grads(s):
        g[s, 2] = (acc[s, 0] * FACTOR).astype(BF16)
        g[s, 3] = acc[s, 1].astype(BF16)
        send_back(s, 1)

    def later_step(s, _):
        await_mate(s)
        for i in range(2):
            within(s, i, [(z[s, 1], z[s, 0], None)], True)
        remote(stats.at[s], stats_in.at[s], l_s.at[s], l_r.at[s], mate).start()
        send_back(s, 0)
        put_key_grads(s)
        return 0

    def earlier_step(s, _):
        await_mate(s)
        await_bytes(stats_in.at[s], l_r.at[s])
        k, v = t[s, 1], t[s, 2]
        for i in range(2):
            rows = pl.ds(i * 256, 256)
            q, do = z[s, 1, rows], z[s, 0, rows]
            prob = jnp.exp(dot_t(k, q) * FACTOR - stats_in[s, 0:1, rows])
            grad = (prob * (dot_t(v, do) - stats_in[s, 1:2, rows])).astype(BF16)
            acc[s, 0] = acc[s, 0] + dot(grad, q)
            acc[s, 1] = acc[s, 1] + dot(prob.astype(BF16), do)
        put_key_grads(s)
        return 0

    @pl.when(par == 0)
    def _():
        lax.fori_loop(0, count, earlier_step, 0)

    @pl.when(par == 1)
    def _():
        lax.fori_loop(0, count, later_step, 0)

    await_bytes(rim_in, m_r.at[2])

    def fold_step(j, sums_so_far):
        cols = columns(j)
        low = pl.ds(ROWS - DOC_MAX, DOC_MAX)
        sd[1, low, cols] = sd[1, low, cols] + rim_in[0, :, cols].astype(F32)
        sd[2, low, cols] = sd[2, low, cols] + rim_in[1, :, cols].astype(F32)
        fin[5, :, cols] = sd[2, :, cols].astype(BF16)
        a, b = sums_so_far
        a = a + sd[0, :, cols] * gains[0:1, cols] * raw[2, :, cols].astype(F32)
        b = b + sd[1, :, cols] * gains[1:2, cols] * raw[3, :, cols].astype(F32)
        return a, b

    short_sums = lax.fori_loop(0, HEADS, fold_step, (zero, zero))

    def await_back(pair, s, d):
        await_bytes(r.at[pl.ds(2 * pair, 2), :, columns(0)], b_r.at[pair, s, d])

    for pair in range(2):
        for s in range(3):
            for d in range(4):
                if s < 2:
                    await_back(pair, s, d)
                else:
                    pl.when(has_third(x_at(4 - d), core))(
                        lambda pair=pair, s=s, d=d: await_back(pair, s, d)
                    )
    pltpu.make_async_copy(r.at[0], lout, o_s.at[1]).start()
    pltpu.make_async_copy(r.at[3], ldqkv.at[2], o_s.at[2]).start()
    pltpu.make_async_copy(fin.at[5], sdqkv.at[2], o_s.at[3]).start()

    def inner_step(j, sums_so_far):
        cols = columns(j)
        a, b = sums_so_far
        a = a + r[1, :, cols].astype(F32) * gains[0:1, cols] * raw[0, :, cols].astype(F32)
        b = b + r[2, :, cols].astype(F32) * gains[1:2, cols] * raw[1, :, cols].astype(F32)
        return a, b

    long_sums = lax.fori_loop(0, HEADS, inner_step, (zero, zero))
    sums[1] = to_rows([jnp.sum(a, axis=1, keepdims=True) for a in (*long_sums, *short_sums)])
    for d in (1, 2, 3):
        remote(sums.at[1], sums_in.at[1, d], h_s.at[1, d], h_r.at[1, d], head_dev(d)).start()
    for d in (1, 2, 3):
        await_bytes(sums_in.at[1, d], h_r.at[1, d])
    inner = to_cols((sums[1] + sums_in[1, 1] + sums_in[1, 2] + sums_in[1, 3]) / WIDTH)
    scale = inv[...]
    pull = scale * scale * scale * inner

    def final_step(j, _):
        cols = columns(j)
        grads = (r[1, :, cols].astype(F32), r[2, :, cols].astype(F32), sd[0, :, cols], sd[1, :, cols])
        for i in range(4):
            fin[i, :, cols] = (
                scale[:, i : i + 1] * gains[i % 2 : i % 2 + 1, cols] * grads[i]
                - raw[i, :, cols].astype(F32) * pull[:, i : i + 1]
            ).astype(BF16)
        return 0

    lax.fori_loop(0, HEADS, final_step, 0)
    pltpu.make_async_copy(fin.at[pl.ds(0, 2)], ldqkv.at[pl.ds(0, 2)], o_s.at[4]).start()
    pltpu.make_async_copy(fin.at[pl.ds(2, 2)], sdqkv.at[pl.ds(0, 2)], o_s.at[5]).start()

    def left_values(s, d):
        await_bytes(t.at[s, 2, mine], v_s.at[0, s, d])
        await_bytes(t.at[s, 3, mine], v_s.at[1, s, d])
        await_bytes(t.at[s, pl.ds(0, 2), mine], q_s.at[s, d])

    for s in range(3):
        to_peers(s, left_values)

    def left_step(s, _):
        for d in range(4):
            await_bytes(t.at[s, 0, mine], z_s.at[0, s, d])
            await_bytes(t.at[s, 0, mine], z_s.at[1, s, d])
        for d in (1, 2, 3):
            await_bytes(g.at[s, pl.ds(0, 2), mine], b_s.at[0, s, d])
            await_bytes(g.at[s, pl.ds(0, 2), mine], b_s.at[1, s, d])
        pl.when(par == 1)(lambda: await_bytes(stats.at[s], l_s.at[s]))
        return 0

    lax.fori_loop(0, count, left_step, 0)
    for phase in range(2):
        for d in (1, 2, 3):
            await_bytes(sums.at[phase], h_s.at[phase, d])
    await_bytes(vx.at[pl.ds(0, DOC_MAX)], m_s.at[0])
    await_bytes(kx.at[pl.ds(0, DOC_MAX)], m_s.at[1])
    await_bytes(rim_out, m_s.at[2])
    await_bytes(so, o_s.at[0])
    await_bytes(r.at[0], o_s.at[1])
    await_bytes(r.at[3], o_s.at[2])
    await_bytes(fin.at[5], o_s.at[3])
    await_bytes(fin.at[pl.ds(0, 2)], o_s.at[4])
    await_bytes(fin.at[pl.ds(2, 2)], o_s.at[5])


def on_device(long_qkv, long_grad, short_qkv, short_grad, short_lengths, norm_gains):
    anywhere = pl.BlockSpec(memory_space=pl.ANY)
    vmem = pl.BlockSpec(memory_space=pltpu.VMEM)
    wide = (ROWS, LOCAL)
    dma = pltpu.SemaphoreType.DMA
    return pl.pallas_call(
        kernel,
        out_shape=(
            jax.ShapeDtypeStruct(wide, BF16),
            jax.ShapeDtypeStruct((3, *wide), BF16),
            jax.ShapeDtypeStruct(wide, BF16),
            jax.ShapeDtypeStruct((3, *wide), BF16),
        ),
        in_specs=[anywhere] * 4 + [vmem] * 2,
        out_specs=(anywhere,) * 4,
        scratch_shapes=[
            pltpu.VMEM((4, *wide), BF16),
            pltpu.VMEM((2, *wide), BF16),
            pltpu.VMEM(wide, BF16),
            pltpu.VMEM((ROWS + DOC_MAX, LOCAL), BF16),
            pltpu.VMEM((ROWS + DOC_MAX, LOCAL), BF16),
            pltpu.VMEM(wide, BF16),
            pltpu.VMEM((ROWS, HEAD_DIM), F32),
            pltpu.VMEM((2, 8, HEAD_DIM), F32),
            pltpu.VMEM((2, 4, 8, HEAD_DIM), F32),
            pltpu.VMEM((3, 4, HALF, HEAD_DIM), BF16),
            pltpu.VMEM((3, 2, HALF, HEAD_DIM), BF16),
            pltpu.VMEM((3, 8, HALF), F32),
            pltpu.VMEM((3, 8, HALF), F32),
            pltpu.VMEM((3, 4, HALF, HEAD_DIM), BF16),
            pltpu.VMEM((3, 2, HALF, HEAD_DIM), F32),
            pltpu.VMEM((4, *wide), BF16),
            pltpu.VMEM(wide, BF16),
            pltpu.VMEM((3, *wide), F32),
            pltpu.VMEM((2, DOC_MAX, LOCAL), BF16),
            pltpu.VMEM((2, DOC_MAX, LOCAL), BF16),
            pltpu.VMEM((6, *wide), BF16),
            dma((6,)),
            dma((2, 3, 4)),
            dma((2, 3, 4)),
            dma((3, 4)),
            dma((3, 4)),
            dma((2, 3, 4)),
            dma((2, 3, 4)),
            dma((3,)),
            dma((3,)),
            dma((2, 3, 4)),
            dma((2, 3, 4)),
            dma((2, 4)),
            dma((2, 4)),
            dma((3,)),
            dma((3,)),
            dma((6,)),
        ],
        compiler_params=pltpu.CompilerParams(
            collective_id=0, has_side_effects=True, vmem_limit_bytes=50 * 2**20
        ),
    )(long_qkv, long_grad, short_qkv, short_grad, short_lengths.reshape(1, -1), norm_gains)


def solution(mesh):
    return jax.shard_map(
        on_device,
        mesh=mesh,
        in_specs=(
            P(None, "ctx", "head"),
            P("ctx", "head"),
            P(None, "ctx", "head"),
            P("ctx", "head"),
            P(),
            P(None, "head"),
        ),
        out_specs=(
            P("ctx", "head"),
            P(None, "ctx", "head"),
            P("ctx", "head"),
            P(None, "ctx", "head"),
        ),
        check_vma=False,
    )
```

time: 678 us -> 84.2 us (0.12)
  the two profiles are of different devices: /device:TPU:86 before, /device:TPU:37 now
where the time goes in v1:
time: 84.2 us; the launch traced here: 84 us
  Pallas kernels  76.7 us (91%)
  local copies, waits for them, and re-layouts  6.66 us (8%)
    pallas_call x1, Pallas kernels, on_device(): pl.pallas_call(kernel, out_shape=(jax.ShapeDtypeStruct(wide, BF16), jax.S...  76.7 us
    unnamed x12, local copies, waits for them, and re-layouts  6.66 us

profile of v1, /device:TPU:37, one launch (start us, length us, event | category | flops | bytes accessed | tf_op | source)
XLA Modules:
  0.0 84.0 jit_solution(8038464638421397440)
XLA Ops:
  0.6 0.0 copy-start.3
  0.6 0.7 copy-done.3
  1.3 0.0 copy-start
  1.3 1.0 %copy-done = bf16[128,1280]{1,0:T(8,128)(2,1)S(1)} copy-done((bf16[128,1280]{1,0:T(8,128)(2,1)S(1)}, bf16[128,1280]{1,0:T(8,128)(2,1)}, u32[]{:S(2)}) %copy-start) | copy-done | bytes 327704
  2.3 0.0 copy-start.1
  2.3 1.0 %copy-done.1 = bf16[128,1280]{1,0:T(8,128)(2,1)S(1)} copy-done((bf16[128,1280]{1,0:T(8,128)(2,1)S(1)}, bf16[128,1280]{1,0:T(8,128)(2,1)}, u32[]{:S(2)}) %copy-start.1) | copy-done | bytes 327704
  3.3 0.0 copy-start.2
  3.3 0.7 copy-done.2
  4.0 76.7 %shard_map.93 = (bf16[128,1280]{1,0:T(8,128)(2,1)S(1)}, bf16[3,128,1280]{2,1,0:T(8,128)(2,1)S(1)}, bf16[128,1280]{1,0:T(8,128)(2,1)S(1)}, bf16[3,128,1280]{2,1,0:T(8,128)(2,1)S(1)}) custom-call(bf16[3,128,1280]{2,1,0:T(8,128)(2,1)} %lqkv.1, bf16[128,1280]{1,0:T(8,128)(2,1)S(1)} %copy-done, bf16[3,128,1280]{2,1,0:T(8,128)(2,1)} %sqkv.1, ...), custom_call_target="tpu_custom_call" | custom-call | tf_op jit(solution)/shard_map/pallas_call | solution.py:468
  80.7 0.7 copy.14
  81.4 0.9 %copy.15 = bf16[3,128,1280]{2,1,0:T(8,128)(2,1)} copy(bf16[3,128,1280]{2,1,0:T(8,128)(2,1)S(1)} %get-tuple-element.9) | data formatting | bytes 1966080
  82.3 0.7 copy.16
  83.1 0.9 %copy.17 = bf16[3,128,1280]{2,1,0:T(8,128)(2,1)} copy(bf16[3,128,1280]{2,1,0:T(8,128)(2,1)S(1)} %get-tuple-element.11) | data formatting | bytes 1966080
Async XLA Ops:
  0.6 0.7 copy-start.3
  1.3 1.0 %copy-start = (bf16[128,1280]{1,0:T(8,128)(2,1)S(1)}, bf16[128,1280]{1,0:T(8,128)(2,1)}, u32[]{:S(2)}) copy-start(bf16[128,1280]{1,0:T(8,128)(2,1)} %lgrad.1) | copy-start | bytes 983044
  2.3 1.0 %copy-start.1 = (bf16[128,1280]{1,0:T(8,128)(2,1)S(1)}, bf16[128,1280]{1,0:T(8,128)(2,1)}, u32[]{:S(2)}) copy-start(bf16[128,1280]{1,0:T(8,128)(2,1)} %sgrad.1) | copy-start | bytes 983044
  3.3 0.7 copy-start.2

commit v2 on v1

v2 whole, which is shorter than its diff:
```python
import jax
import jax.numpy as jnp
from jax import lax
from jax.experimental import pallas as pl
from jax.experimental.pallas import tpu as pltpu
from jax.sharding import PartitionSpec as P

MESH = pl.DeviceIdType.MESH
BF16 = jnp.bfloat16
F32 = jnp.float32
HEAD_DIM = 128
WIDTH = 5120
DOC_MAX = 64
STRIP = 16
PIECE = 640
WAVE = 5
ROWS = 128
LOCAL = 1280
HEADS = 10
HALF = 512
EPSILON = 1e-06
NEGATIVE = -1e30
FACTOR = HEAD_DIM ** (-0.5)


def first_head(x, core):
    return lax.div(5 * x + 1 - core, 2)


def has_third(x, core):
    return lax.rem(x + core, 2) == 0


def columns(head):
    return pl.ds(pl.multiple_of(head * HEAD_DIM, HEAD_DIM), HEAD_DIM)


def block_rows(x):
    return pl.ds(pl.multiple_of(x * ROWS, ROWS), ROWS)


def await_bytes(ref, sem):
    pltpu.make_async_copy(ref, ref, sem).wait()


def dot(a, b):
    return jnp.dot(a, b, preferred_element_type=F32)


def dot_t(a, b):
    return lax.dot_general(a, b, (((1,), (1,)), ((), ())), preferred_element_type=F32)


def sweep(step, carry):
    def group(i, c):
        for j in range(WAVE):
            c = step(i * WAVE + j, c)
        return c

    return lax.fori_loop(0, HEADS // WAVE, group, carry)


def attend(items):
    scores = []
    for q, _, pieces in items:
        row = []
        for k, _, mask in pieces:
            one = dot_t(k, q) * FACTOR
            row.append(one if mask is None else jnp.where(mask, one, NEGATIVE))
        scores.append(row)
    slopes = [[dot_t(v, do) for _, v, _ in pieces] for _, do, pieces in items]
    highs, totals, probs = [], [], []
    for row in scores:
        high = jnp.max(row[0], axis=0, keepdims=True)
        for one in row[1:]:
            high = jnp.maximum(high, jnp.max(one, axis=0, keepdims=True))
        highs.append(high)
    powers = [[jnp.exp(one - high) for one in row] for row, high in zip(scores, highs)]
    for row in powers:
        total = jnp.sum(row[0], axis=0, keepdims=True)
        for one in row[1:]:
            total = total + jnp.sum(one, axis=0, keepdims=True)
        totals.append(total)
    log_totals = [high + jnp.log(total) for high, total in zip(highs, totals)]
    shares = [1.0 / total for total in totals]
    probs = [[one * share for one in row] for row, share in zip(powers, shares)]
    weights = [[one.astype(BF16) for one in row] for row in probs]
    outs_t = []
    for (_, _, pieces), row in zip(items, weights):
        out_t = dot(pieces[0][1].T, row[0])
        for (_, v, _), one in zip(pieces[1:], row[1:]):
            out_t = out_t + dot(v.T, one)
        outs_t.append(out_t.astype(BF16))
    outs = [out_t.astype(F32).T.astype(BF16) for out_t in outs_t]
    row_dots = [
        jnp.sum(do.astype(F32).T * out_t.astype(F32), axis=0, keepdims=True)
        for (_, do, _), out_t in zip(items, outs_t)
    ]
    grads = [
        [(one * (slope - row_dot)).astype(BF16) for one, slope in zip(row, slope_row)]
        for row, slope_row, row_dot in zip(probs, slopes, row_dots)
    ]
    dqs = []
    for (_, _, pieces), row in zip(items, grads):
        dq_t = dot(pieces[0][0].T, row[0])
        for (k, _, _), one in zip(pieces[1:], row[1:]):
            dq_t = dq_t + dot(k.T, one)
        dqs.append((dq_t * FACTOR).T)
    return outs, dqs, log_totals, row_dots, weights, grads


def to_rows(cols):
    lane = lax.broadcasted_iota(jnp.int32, (ROWS, HEAD_DIM), 1)
    packed = jnp.zeros((ROWS, HEAD_DIM), F32)
    for i, col in enumerate(cols):
        packed = jnp.where(lane == i, col, packed)
    return packed.T[:8]


def to_cols(rows):
    return jnp.concatenate([rows] * (ROWS // 8), axis=0).T


def kernel(
    lqkv, lgrad, sqkv, sgrad, lengths, gains,
    lout, ldqkv, sout, sdqkv,
    raw, nlong, w, hops, lens, gain, inv, sums, sums_in,
    t, z, stats, stats_in, g, acc, r, so, sd, edge, edge_in, fin,
    load, v_s, v_r, q_s, q_r, z_s, z_r, l_s, l_r, b_s, b_r, h_s, h_r, m_s, m_r, p_s, p_r, f_s, f_r, e_sem, o_s,
):
    c = lax.axis_index("ctx")
    h = lax.axis_index("head")
    x = lax.rem(c, 4)
    row_base = c - x
    par = lax.rem(lax.div(c, 4), 2)
    core = lax.rem(h, 2)
    third = has_third(x, core)
    count = jnp.where(third, 3, 2)
    first = first_head(x, core)
    mate = (c + 4 - 8 * par, h)
    after = (lax.rem(c + 1, 64), h)
    before = (lax.rem(c + 63, 64), h)

    def x_at(d):
        return lax.rem(x + d, 4)

    def x_dev(d):
        return (row_base + x_at(d), h)

    def head_dev(d):
        return (c, lax.rem(h + d, 4))

    def remote(src, dst, send, recv, dev):
        return pltpu.make_async_remote_copy(
            src_ref=src, dst_ref=dst, send_sem=send, recv_sem=recv,
            device_id=dev, device_id_type=MESH,
        )

    loads = [
        pltpu.make_async_copy(lqkv.at[0], raw.at[0], load.at[0]),
        pltpu.make_async_copy(lqkv.at[1], raw.at[1], load.at[1]),
        pltpu.make_async_copy(sqkv.at[0], raw.at[2], load.at[2]),
        pltpu.make_async_copy(sqkv.at[1], raw.at[3], load.at[3]),
        pltpu.make_async_copy(gains, gain, load.at[4]),
        pltpu.make_async_copy(sqkv.at[2], w.at[0, 1, pl.ds(DOC_MAX, ROWS)], load.at[5]),
        pltpu.make_async_copy(sgrad, w.at[1, 1, pl.ds(0, ROWS)], load.at[6]),
        pltpu.make_async_copy(lengths, lens, load.at[7]),
    ]
    for copy in loads:
        copy.start()

    peers = [x_dev(1), x_dev(2), x_dev(3), mate, head_dev(1), head_dev(2), head_dev(3), after, before]
    barrier = pltpu.get_barrier_semaphore()
    for dev in peers:
        pl.semaphore_signal(barrier, inc=1, device_id=dev, device_id_type=MESH)

    mine = block_rows(x)

    def own_values(s):
        for kind, src in ((0, lqkv.at[2]), (1, lgrad)):
            pltpu.make_async_copy(
                src.at[:, columns(first + s)], t.at[s, 2 + kind, mine], v_r.at[kind, s, 0]
            ).start()

    def send_values(s, d):
        for kind, src in ((0, lqkv.at[2]), (1, lgrad)):
            remote(
                src.at[:, columns(first_head(x_at(d), core) + s)], t.at[s, 2 + kind, mine],
                v_s.at[kind, s, d], v_r.at[kind, s, d], x_dev(d),
            ).start()

    def send_keys(s, d):
        remote(
            nlong.at[:, :, columns(first_head(x_at(d), core) + s)], t.at[s, pl.ds(0, 2), mine],
            q_s.at[s, d], q_r.at[s, d], x_dev(d),
        ).start()

    def own_keys(s):
        pltpu.make_async_copy(
            nlong.at[:, :, columns(first + s)], t.at[s, pl.ds(0, 2), mine], q_r.at[s, 0]
        ).start()

    def to_peers(s, send):
        for d in (1, 2, 3):
            if s < 2:
                send(s, d)
            else:
                pl.when(has_third(x_at(d), core))(lambda d=d: send(s, d))

    own_values(0)
    own_values(1)
    pl.when(third)(lambda: own_values(2))

    pl.semaphore_wait(barrier, len(peers))

    to_peers(0, send_values)

    base = ROWS * (1 - par)
    ending = x == 3 - 3 * par
    inner_column = jnp.logical_not(ending)
    meeting = x == 3 * par
    sends_on = jnp.logical_not((par == 0) & (x == 3))
    sends_back = jnp.logical_not((par == 1) & (x == 0))
    last = far = pl.ds(ROWS, DOC_MAX)
    near = pl.ds(0, DOC_MAX)

    def strip(column):
        return pl.ds(pl.multiple_of(base + column * STRIP, STRIP), STRIP)

    def send_rims(part):
        @pl.when(ending)
        def _():
            for d in (1, 2, 3):
                remote(
                    w.at[par, part, strip(x_at(d))], hops.at[part, 0],
                    p_s.at[part, d], p_r.at[part, 0], x_dev(d),
                ).start()
            remote(
                w.at[par, part, strip(x)], hops.at[part, 1], p_s.at[part, 0], p_r.at[part, 1], mate
            ).start()

        @pl.when(sends_on)
        def _():
            remote(
                w.at[0, part, last], w.at[0, part, near], m_s.at[part, 0], m_r.at[part, 0], after
            ).start()

        @pl.when(sends_back)
        def _():
            remote(
                w.at[1, part, near], w.at[1, part, far], m_s.at[part, 1], m_r.at[part, 1], before
            ).start()

    def cross_rims(part):
        @pl.when(inner_column)
        def _():
            await_bytes(hops.at[part, 0], p_r.at[part, 0])

            @pl.when(meeting)
            def _():
                there = pl.ds(pl.multiple_of(ROWS * par + x * STRIP, STRIP), STRIP)
                remote(
                    hops.at[part, 0], w.at[par, part, there],
                    p_s.at[part, 0], f_r.at[part, 0], mate,
                ).start()

            @pl.when(jnp.logical_not(meeting))
            def _():
                remote(
                    hops.at[part, 0], hops.at[part, 1], p_s.at[part, 0], p_r.at[part, 1], mate
                ).start()

    def land_rims(part):
        @pl.when(inner_column)
        def _():
            await_bytes(hops.at[part, 1], p_r.at[part, 1])
            end_d = lax.rem(3 - 3 * par + 4 - x, 4)
            end_dev = (row_base + 3 - 3 * par, h)
            remote(
                hops.at[part, 1], w.at[1 - par, part, strip(x)],
                f_s.at[part], f_r.at[part, end_d], end_dev,
            ).start()

    for copy in loads[5:7]:
        copy.wait()
    send_rims(1)
    to_peers(1, send_values)

    def relay_values(s, d):
        rows = block_rows(lax.rem(x + 4 - d, 4))
        await_bytes(t.at[s, 2, rows], v_r.at[0, s, d])
        await_bytes(t.at[s, 3, rows], v_r.at[1, s, d])
        remote(t.at[s, 2 + par, rows], z.at[s, 0, rows], z_s.at[0, s, d], z_r.at[0, s, d], mate).start()

    def relay_keys(s, d):
        rows = block_rows(lax.rem(x + 4 - d, 4))
        await_bytes(t.at[s, pl.ds(0, 2), rows], q_r.at[s, d])
        remote(t.at[s, 1 - par, rows], z.at[s, 1, rows], z_s.at[1, s, d], z_r.at[1, s, d], mate).start()

    relay_values(0, 0)
    relay_values(1, 0)
    pl.when(third)(lambda: relay_values(2, 0))

    for copy in loads[:5]:
        copy.wait()

    def square_step(j, sums_so_far):
        cols = columns(j)
        new = []
        for i in range(4):
            wide = raw[i, :, cols].astype(F32)
            new.append(sums_so_far[i] + wide * wide)
        return tuple(new)

    zero = jnp.zeros((ROWS, HEAD_DIM), F32)
    squares = sweep(square_step, (zero,) * 4)
    sums[0] = to_rows([jnp.sum(a, axis=1, keepdims=True) for a in squares])
    for d in (1, 2, 3):
        remote(sums.at[0], sums_in.at[0, d], h_s.at[0, d], h_r.at[0, d], head_dev(d)).start()
    for d in (1, 2, 3):
        relay_values(0, d)
    cross_rims(1)
    for d in (1, 2, 3):
        await_bytes(sums_in.at[0, d], h_r.at[0, d])
    all_sums = sums[0] + sums_in[0, 1] + sums_in[0, 2] + sums_in[0, 3]
    inv[...] = to_cols(lax.rsqrt(all_sums / WIDTH + EPSILON))

    spread = [jnp.broadcast_to(inv[:, i : i + 1], (ROWS, HEAD_DIM)) for i in range(4)]

    def normalize_step(j, _):
        cols = columns(j)
        nlong[0, :, cols] = (raw[0, :, cols].astype(F32) * spread[0] * gain[0:1, cols]).astype(BF16)
        nlong[1, :, cols] = (raw[1, :, cols].astype(F32) * spread[1] * gain[1:2, cols]).astype(BF16)
        w[1, 0, pl.ds(0, ROWS), cols] = (
            raw[2, :, cols].astype(F32) * spread[2] * gain[0:1, cols]
        ).astype(BF16)
        w[0, 0, pl.ds(DOC_MAX, ROWS), cols] = (
            raw[3, :, cols].astype(F32) * spread[3] * gain[1:2, cols]
        ).astype(BF16)
        return 0

    sweep(normalize_step, 0)

    send_rims(0)
    own_keys(0)
    own_keys(1)
    pl.when(third)(lambda: own_keys(2))
    to_peers(0, send_keys)
    to_peers(1, send_keys)
    to_peers(2, send_values)
    to_peers(2, send_keys)
    for d in (1, 2, 3):
        relay_values(1, d)
    cross_rims(0)

    diag = lax.broadcasted_iota(jnp.int32, (256, 256), 0) <= lax.broadcasted_iota(
        jnp.int32, (256, 256), 1
    )

    def send_back(s, pair):
        for d in (1, 2, 3):
            remote(
                g.at[s, pl.ds(2 * pair, 2), block_rows(x_at(d))],
                r.at[pl.ds(2 * pair, 2), :, columns(first + s)],
                b_s.at[pair, s, d], b_r.at[pair, s, d], x_dev(d),
            ).start()
        pltpu.make_async_copy(
            g.at[s, pl.ds(2 * pair, 2), mine], r.at[pl.ds(2 * pair, 2), :, columns(first + s)],
            b_r.at[pair, s, 0],
        ).start()

    def within(s, early, keep):
        low, high = pl.ds(0, 256), pl.ds(256, 256)
        pair = [(t[s, 0, rows], t[s, 3, rows]) for rows in (low, high)]
        k_low, v_low = t[s, 1, low], t[s, 2, low]
        items = [
            (*pair[0], [*early, (k_low, v_low, diag)]),
            (*pair[1], [*early, (k_low, v_low, None), (t[s, 1, high], t[s, 2, high], diag)]),
        ]
        outs, dqs, log_totals, row_dots, weights, grads = attend(items)
        for i, rows in enumerate((low, high)):
            g[s, 0, rows] = outs[i]
            g[s, 1, rows] = dqs[i].astype(BF16)
            if keep:
                stats[s, 0:1, rows] = log_totals[i]
                stats[s, 1:2, rows] = row_dots[i]
        at = len(early)
        acc[s, 0, low] = dot(grads[0][at], pair[0][0]) + dot(grads[1][at], pair[1][0])
        acc[s, 1, low] = dot(weights[0][at], pair[0][1]) + dot(weights[1][at], pair[1][1])
        acc[s, 0, high] = dot(grads[1][-1], pair[1][0])
        acc[s, 1, high] = dot(weights[1][-1], pair[1][1])

    def first_half(s):
        @pl.when(par == 0)
        def _():
            within(s, [], False)
            send_back(s, 0)

    def relay_all_keys(s):
        for d in range(4):
            relay_keys(s, d)

    relay_all_keys(0)
    land_rims(1)
    first_half(0)
    relay_all_keys(1)
    land_rims(0)
    first_half(1)

    loads[7].wait()
    docs = lens.shape[1]

    def short_documents():
        for part in range(2):

            @pl.when(sends_back)
            def _():
                await_bytes(w.at[0, part, near], m_r.at[part, 0])

            @pl.when(ending & (par == 1))
            def _():
                for d in range(4):
                    await_bytes(w.at[0, part, pl.ds(0, STRIP)], f_r.at[part, d])

        def short_step(i, _):
            spans = [columns(i * WAVE + j) for j in range(WAVE)]
            own = pl.ds(0, ROWS)
            items = [
                (w[1, 0, own, cols], w[1, 1, own, cols], [(w[0, 0, :, cols], w[0, 1, :, cols], allowed)])
                for cols in spans
            ]
            outs, dqs, log_totals, row_dots, weights, grads = attend(items)
            dks = [dot(grad[0][DOC_MAX:], item[0]) * FACTOR for grad, item in zip(grads, items)]
            dvs = [dot(weight[0][DOC_MAX:], item[1]) for weight, item in zip(weights, items)]
            for j, cols in enumerate(spans):
                so[:, cols] = outs[j]
                sd[0, :, cols] = dqs[j]
                sd[1, :, cols] = dks[j]
                sd[2, :, cols] = dvs[j]
                edge[i * WAVE + j, 0:1] = log_totals[j]
                edge[i * WAVE + j, 1:2] = row_dots[j]
            return 0

        lax.fori_loop(0, HEADS // WAVE, short_step, 0)
        remote(edge, edge_in, e_sem.at[0], e_sem.at[1], before).start()
        pltpu.make_async_copy(so, sout, o_s.at[0]).start()

    def document_begins(first_query, queries):
        query_pos = first_query + lax.broadcasted_iota(jnp.int32, (1, queries), 1)
        return query_pos, jnp.max(jnp.where(ends <= query_pos, ends, 0), axis=0, keepdims=True)

    until = lax.broadcasted_iota(jnp.int32, (docs, docs), 1) <= lax.broadcasted_iota(
        jnp.int32, (docs, docs), 0
    )
    ends = jnp.sum(jnp.where(until, lens[...], 0), axis=1, keepdims=True)
    query_pos, begin = document_begins(c * ROWS, ROWS)
    key_pos = c * ROWS - DOC_MAX + lax.broadcasted_iota(jnp.int32, (ROWS + DOC_MAX, ROWS), 0)
    allowed = (key_pos <= query_pos) & (key_pos >= begin)

    def await_mate(s):
        for d in range(4):
            rows = block_rows(lax.rem(x + 4 - d, 4))
            await_bytes(z.at[s, 0, rows], z_r.at[0, s, d])
            await_bytes(z.at[s, 1, rows], z_r.at[1, s, d])

    def put_key_grads(s):
        g[s, 2] = (acc[s, 0] * FACTOR).astype(BF16)
        g[s, 3] = acc[s, 1].astype(BF16)
        send_back(s, 1)

    def later_step(s):
        await_mate(s)
        within(s, [(z[s, 1], z[s, 0], None)], True)
        remote(stats.at[s], stats_in.at[s], l_s.at[s], l_r.at[s], mate).start()
        send_back(s, 0)
        put_key_grads(s)

    def earlier_step(s):
        await_mate(s)
        await_bytes(stats_in.at[s], l_r.at[s])
        k, v = t[s, 1], t[s, 2]
        for i in range(2):
            rows = pl.ds(i * 256, 256)
            q, do = z[s, 1, rows], z[s, 0, rows]
            prob = jnp.exp(dot_t(k, q) * FACTOR - stats_in[s, 0:1, rows])
            grad = (prob * (dot_t(v, do) - stats_in[s, 1:2, rows])).astype(BF16)
            acc[s, 0] = acc[s, 0] + dot(grad, q)
            acc[s, 1] = acc[s, 1] + dot(prob.astype(BF16), do)
        put_key_grads(s)

    def meet(s):
        pl.when(par == 0)(lambda: earlier_step(s))
        pl.when(par == 1)(lambda: later_step(s))

    short_documents()
    pl.when(par == 1)(lambda: later_step(0))

    @pl.when(third)
    def _():
        for d in (1, 2, 3):
            relay_values(2, d)
        relay_all_keys(2)
        first_half(2)

    pl.when(par == 0)(lambda: earlier_step(0))
    meet(1)

    for part in range(2):

        @pl.when(sends_on)
        def _():
            await_bytes(w.at[1, part, far], m_r.at[part, 1])

        @pl.when(ending & (par == 0))
        def _():
            for d in range(4):
                await_bytes(w.at[1, part, pl.ds(0, STRIP)], f_r.at[part, d])

    await_bytes(edge_in, e_sem.at[1])
    next_begin = document_begins((c + 1) * ROWS, ROWS)[1]
    last_pos = c * ROWS + ROWS - DOC_MAX + lax.broadcasted_iota(jnp.int32, (DOC_MAX, DOC_MAX), 0)
    reached = last_pos >= next_begin[:, :DOC_MAX]

    def fold_step(i, sums_so_far):
        low = pl.ds(ROWS - DOC_MAX, DOC_MAX)
        lanes = pl.ds(0, DOC_MAX)
        spans = [columns(i * WAVE + j) for j in range(WAVE)]
        keys = [(w[0, 0, last, cols], w[0, 1, last, cols]) for cols in spans]
        queries = [(w[1, 0, far, cols], w[1, 1, far, cols]) for cols in spans]
        scores = [dot_t(k, q) * FACTOR for (k, _), (q, _) in zip(keys, queries)]
        slopes = [dot_t(v, do) for (_, v), (_, do) in zip(keys, queries)]
        probs = [
            jnp.where(reached, jnp.exp(one - edge_in[i * WAVE + j, 0:1, lanes]), 0.0)
            for j, one in enumerate(scores)
        ]
        grads = [
            (prob * (slope - edge_in[i * WAVE + j, 1:2, lanes])).astype(BF16)
            for j, (prob, slope) in enumerate(zip(probs, slopes))
        ]
        dks = [dot(grad, q) * FACTOR for grad, (q, _) in zip(grads, queries)]
        dvs = [dot(prob.astype(BF16), do) for prob, (_, do) in zip(probs, queries)]
        a, b = sums_so_far
        for j, cols in enumerate(spans):
            sd[1, low, cols] = sd[1, low, cols] + dks[j]
            sd[2, low, cols] = sd[2, low, cols] + dvs[j]
        for cols in spans:
            fin[5, :, cols] = sd[2, :, cols].astype(BF16)
            a = a + sd[0, :, cols] * gain[0:1, cols] * raw[2, :, cols].astype(F32)
            b = b + sd[1, :, cols] * gain[1:2, cols] * raw[3, :, cols].astype(F32)
        return a, b

    short_sums = lax.fori_loop(0, HEADS // WAVE, fold_step, (zero, zero))
    pltpu.make_async_copy(fin.at[5], sdqkv.at[2], o_s.at[3]).start()

    def start_inner(phase, pair):
        sums[phase] = to_rows([jnp.sum(a, axis=1, keepdims=True) for a in pair])
        for d in (1, 2, 3):
            remote(
                sums.at[phase], sums_in.at[phase, d], h_s.at[phase, d], h_r.at[phase, d], head_dev(d)
            ).start()

    def end_inner(phase, at, grads):
        for d in (1, 2, 3):
            await_bytes(sums_in.at[phase, d], h_r.at[phase, d])
        inner = to_cols(
            (sums[phase] + sums_in[phase, 1] + sums_in[phase, 2] + sums_in[phase, 3]) / WIDTH
        )

        scales = [jnp.broadcast_to(inv[:, at + i : at + i + 1], (ROWS, HEAD_DIM)) for i in range(2)]
        pulls = [
            scale * scale * scale * jnp.broadcast_to(inner[:, i : i + 1], (ROWS, HEAD_DIM))
            for i, scale in enumerate(scales)
        ]

        def final_step(j, _):
            cols = columns(j)
            for i in range(2):
                fin[at + i, :, cols] = (
                    scales[i] * gain[i : i + 1, cols] * grads(i, cols)
                    - raw[at + i, :, cols].astype(F32) * pulls[i]
                ).astype(BF16)
            return 0

        sweep(final_step, 0)

    start_inner(1, short_sums)
    pl.when(third)(lambda: meet(2))
    end_inner(1, 2, lambda i, cols: sd[i, :, cols])
    pltpu.make_async_copy(fin.at[pl.ds(2, 2)], sdqkv.at[pl.ds(0, 2)], o_s.at[5]).start()

    def await_back(pair, s, d):
        await_bytes(r.at[pl.ds(2 * pair, 2), :, columns(0)], b_r.at[pair, s, d])

    for pair in range(2):
        for s in range(3):
            for d in range(4):
                if s < 2:
                    await_back(pair, s, d)
                else:
                    pl.when(has_third(x_at(4 - d), core))(
                        lambda pair=pair, s=s, d=d: await_back(pair, s, d)
                    )
    pltpu.make_async_copy(r.at[0], lout, o_s.at[1]).start()
    pltpu.make_async_copy(r.at[3], ldqkv.at[2], o_s.at[2]).start()
    def inner_step(j, sums_so_far):
        cols = columns(j)
        a, b = sums_so_far
        a = a + r[1, :, cols].astype(F32) * gain[0:1, cols] * raw[0, :, cols].astype(F32)
        b = b + r[2, :, cols].astype(F32) * gain[1:2, cols] * raw[1, :, cols].astype(F32)
        return a, b

    long_sums = sweep(inner_step, (zero, zero))
    start_inner(2, long_sums)
    end_inner(2, 0, lambda i, cols: r[1 + i, :, cols].astype(F32))
    pltpu.make_async_copy(fin.at[pl.ds(0, 2)], ldqkv.at[pl.ds(0, 2)], o_s.at[4]).start()

    def left_values(s, d):
        await_bytes(t.at[s, 2, mine], v_s.at[0, s, d])
        await_bytes(t.at[s, 3, mine], v_s.at[1, s, d])
        await_bytes(t.at[s, pl.ds(0, 2), mine], q_s.at[s, d])

    for s in range(3):
        to_peers(s, left_values)

    def left_step(s, _):
        for d in range(4):
            await_bytes(t.at[s, 0, mine], z_s.at[0, s, d])
            await_bytes(t.at[s, 0, mine], z_s.at[1, s, d])
        for d in (1, 2, 3):
            await_bytes(g.at[s, pl.ds(0, 2), mine], b_s.at[0, s, d])
            await_bytes(g.at[s, pl.ds(0, 2), mine], b_s.at[1, s, d])
        pl.when(par == 1)(lambda: await_bytes(stats.at[s], l_s.at[s]))
        return 0

    lax.fori_loop(0, count, left_step, 0)
    for phase in range(3):
        for d in (1, 2, 3):
            await_bytes(sums.at[phase], h_s.at[phase, d])
    for part in range(2):

        @pl.when(sends_on)
        def _():
            await_bytes(w.at[0, part, last], m_s.at[part, 0])

        @pl.when(sends_back)
        def _():
            await_bytes(w.at[1, part, near], m_s.at[part, 1])

        await_bytes(hops.at[part, 0], p_s.at[part, 0])

        @pl.when(ending)
        def _():
            for d in (1, 2, 3):
                await_bytes(hops.at[part, 0], p_s.at[part, d])

        @pl.when(inner_column)
        def _():
            await_bytes(hops.at[part, 1], f_s.at[part])

    await_bytes(edge, e_sem.at[0])
    await_bytes(so, o_s.at[0])
    await_bytes(r.at[0], o_s.at[1])
    await_bytes(r.at[3], o_s.at[2])
    await_bytes(fin.at[5], o_s.at[3])
    await_bytes(fin.at[pl.ds(0, 2)], o_s.at[4])
    await_bytes(fin.at[pl.ds(2, 2)], o_s.at[5])


def hand_over(a, b, c, d, a_out, b_out, c_out, d_out):
    a_out[...] = a[...]
    b_out[...] = b[...]
    c_out[...] = c[...]
    d_out[...] = d[...]


def on_device(long_qkv, long_grad, short_qkv, short_grad, short_lengths, norm_gains):
    anywhere = pl.BlockSpec(memory_space=pl.ANY)
    wide = (ROWS, LOCAL)
    dma = pltpu.SemaphoreType.DMA
    shapes = (
        jax.ShapeDtypeStruct(wide, BF16),
        jax.ShapeDtypeStruct((3, *wide), BF16),
        jax.ShapeDtypeStruct(wide, BF16),
        jax.ShapeDtypeStruct((3, *wide), BF16),
    )
    results = pl.pallas_call(
        kernel,
        out_shape=shapes,
        in_specs=[anywhere] * 6,
        out_specs=(anywhere,) * 4,
        scratch_shapes=[
            pltpu.VMEM((4, *wide), BF16),
            pltpu.VMEM((2, *wide), BF16),
            pltpu.VMEM((2, 2, ROWS + DOC_MAX, LOCAL), BF16),
            pltpu.VMEM((2, 2, STRIP, LOCAL), BF16),
            pltpu.VMEM((1, 256), jnp.int32),
            pltpu.VMEM((2, LOCAL), F32),
            pltpu.VMEM((ROWS, HEAD_DIM), F32),
            pltpu.VMEM((3, 8, HEAD_DIM), F32),
            pltpu.VMEM((3, 4, 8, HEAD_DIM), F32),
            pltpu.VMEM((3, 4, HALF, HEAD_DIM), BF16),
            pltpu.VMEM((3, 2, HALF, HEAD_DIM), BF16),
            pltpu.VMEM((3, 8, HALF), F32),
            pltpu.VMEM((3, 8, HALF), F32),
            pltpu.VMEM((3, 4, HALF, HEAD_DIM), BF16),
            pltpu.VMEM((3, 2, HALF, HEAD_DIM), F32),
            pltpu.VMEM((4, *wide), BF16),
            pltpu.VMEM(wide, BF16),
            pltpu.VMEM((3, *wide), F32),
            pltpu.VMEM((HEADS, 8, ROWS), F32),
            pltpu.VMEM((HEADS, 8, ROWS), F32),
            pltpu.VMEM((6, *wide), BF16),
            dma((8,)),
            dma((2, 3, 4)),
            dma((2, 3, 4)),
            dma((3, 4)),
            dma((3, 4)),
            dma((2, 3, 4)),
            dma((2, 3, 4)),
            dma((3,)),
            dma((3,)),
            dma((2, 3, 4)),
            dma((2, 3, 4)),
            dma((3, 4)),
            dma((3, 4)),
            dma((2, 2)),
            dma((2, 2)),
            dma((2, 4)),
            dma((2, 2)),
            dma((2,)),
            dma((2, 4)),
            dma((2,)),
            dma((6,)),
        ],
        compiler_params=pltpu.CompilerParams(
            collective_id=0, has_side_effects=True, vmem_limit_bytes=60 * 2**20
        ),
    )(long_qkv, long_grad, short_qkv, short_grad, short_lengths.reshape(1, -1), norm_gains)
    flat = pl.BlockSpec((ROWS, PIECE), lambda i: (0, i))
    stacked = pl.BlockSpec((3, ROWS, PIECE), lambda i: (0, 0, i))
    return pl.pallas_call(
        hand_over,
        grid=(LOCAL // PIECE,),
        out_shape=shapes,
        in_specs=[flat, stacked, flat, stacked],
        out_specs=(flat, stacked, flat, stacked),
    )(*results)


def solution(mesh):
    return jax.shard_map(
        on_device,
        mesh=mesh,
        in_specs=(
            P(None, "ctx", "head"),
            P("ctx", "head"),
            P(None, "ctx", "head"),
            P("ctx", "head"),
            P(),
            P(None, "head"),
        ),
        out_specs=(
            P("ctx", "head"),
            P(None, "ctx", "head"),
            P("ctx", "head"),
            P(None, "ctx", "head"),
        ),
        check_vma=False,
    )
```

time: 84.2 us -> 66.8 us (0.79)
  the two profiles are of different devices: /device:TPU:37 before, /device:TPU:1 now
where the time goes in v2:
time: 66.8 us; the launch traced here: 66.6 us
  Pallas kernels  66 us (99%)
    pallas_call x1, Pallas kernels, on_device(): pl.pallas_call(kernel, out_shape=shapes, in_specs=[anywhere] * 6, out_spe...  63.1 us
    pallas_call x1, Pallas kernels, on_device(): pl.pallas_call(hand_over, grid=(LOCAL // PIECE,), out_shape=shapes, in_sp...  2.91 us

profile of v2, /device:TPU:1, one launch (start us, length us, event | category | flops | bytes accessed | tf_op | source)
XLA Modules:
  0.0 66.6 jit_solution(3594523201862547634)
XLA Ops:
  0.6 63.1 %shard_map.93 = (bf16[128,1280]{1,0:T(8,128)(2,1)}, bf16[3,128,1280]{2,1,0:T(8,128)(2,1)}, bf16[128,1280]{1,0:T(8,128)(2,1)}, bf16[3,128,1280]{2,1,0:T(8,128)(2,1)}) custom-call(bf16[3,128,1280]{2,1,0:T(8,128)(2,1)} %lqkv.1, bf16[128,1280]{1,0:T(8,128)(2,1)} %lgrad.1, bf16[3,128,1280]{2,1,0:T(8,128)(2,1)} %sqkv.1, bf16[128,1280]{1,0:T(8,128)(2,1)} %sgrad.1, ...), custom_call_target="tpu_custom_call" | custom-call | tf_op jit(solution)/shard_map/pallas_call | solution.py:686
  63.7 2.9 %shard_map.94 = (bf16[128,1280]{1,0:T(8,128)(2,1)}, bf16[3,128,1280]{2,1,0:T(8,128)(2,1)}, bf16[128,1280]{1,0:T(8,128)(2,1)}, bf16[3,128,1280]{2,1,0:T(8,128)(2,1)}) custom-call(bf16[128,1280]{1,0:T(8,128)(2,1)} %get-tuple-element.8.a, bf16[3,128,1280]{2,1,0:T(8,128)(2,1)} %get-tuple-element.9.b, bf16[128,1280]{1,0:T(8,128)(2,1)} %get-tuple-element.10.c, ...), custom_call_target="tpu_custom_call" | custom-call | tf_op jit(solution)/shard_map/pallas_call | solution.py:741

commit v3 on v2

--- a/solution.py
+++ b/solution.py
@@ -169,10 +169,21 @@
     for copy in loads:
         copy.start()
 
-    peers = [x_dev(1), x_dev(2), x_dev(3), mate, head_dev(1), head_dev(2), head_dev(3), after, before]
+    peers = [x_dev(1), x_dev(2), x_dev(3), mate, head_dev(1), head_dev(2), head_dev(3)]
+    is_first, is_last = c == 0, c == 63
+    leaves = (x == 3) & jnp.logical_not(is_last)
+    enters = (x == 0) & jnp.logical_not(is_first)
     barrier = pltpu.get_barrier_semaphore()
     for dev in peers:
         pl.semaphore_signal(barrier, inc=1, device_id=dev, device_id_type=MESH)
+
+    @pl.when(leaves)
+    def _():
+        pl.semaphore_signal(barrier, inc=1, device_id=after, device_id_type=MESH)
+
+    @pl.when(enters)
+    def _():
+        pl.semaphore_signal(barrier, inc=1, device_id=before, device_id_type=MESH)
 
     mine = block_rows(x)
 
@@ -207,11 +218,20 @@
             else:
                 pl.when(has_third(x_at(d), core))(lambda d=d: send(s, d))
 
+    @pl.when(is_first)
+    def _():
+        w[0, :, pl.ds(0, DOC_MAX)] = jnp.zeros((2, DOC_MAX, LOCAL), BF16)
+
+    @pl.when(is_last)
+    def _():
+        w[1, :, pl.ds(ROWS, DOC_MAX)] = jnp.zeros((2, DOC_MAX, LOCAL), BF16)
+        edge_in[...] = jnp.zeros_like(edge_in)
+
     own_values(0)
     own_values(1)
     pl.when(third)(lambda: own_values(2))
 
-    pl.semaphore_wait(barrier, len(peers))
+    pl.semaphore_wait(barrier, len(peers) + jnp.where(leaves | enters, 1, 0))
 
     to_peers(0, send_values)
 
@@ -219,8 +239,8 @@
     ending = x == 3 - 3 * par
     inner_column = jnp.logical_not(ending)
     meeting = x == 3 * par
-    sends_on = jnp.logical_not((par == 0) & (x == 3))
-    sends_back = jnp.logical_not((par == 1) & (x == 0))
+    sends_on = jnp.logical_not(((par == 0) & (x == 3)) | is_last)
+    sends_back = jnp.logical_not(((par == 1) & (x == 0)) | is_first)
     last = far = pl.ds(ROWS, DOC_MAX)
     near = pl.ds(0, DOC_MAX)
 
@@ -319,7 +339,6 @@
         remote(sums.at[0], sums_in.at[0, d], h_s.at[0, d], h_r.at[0, d], head_dev(d)).start()
     for d in (1, 2, 3):
         relay_values(0, d)
-    cross_rims(1)
     for d in (1, 2, 3):
         await_bytes(sums_in.at[0, d], h_r.at[0, d])
     all_sums = sums[0] + sums_in[0, 1] + sums_in[0, 2] + sums_in[0, 3]
@@ -349,6 +368,7 @@
     to_peers(1, send_keys)
     to_peers(2, send_values)
     to_peers(2, send_keys)
+    cross_rims(1)
     for d in (1, 2, 3):
         relay_values(1, d)
     cross_rims(0)
@@ -407,8 +427,18 @@
     land_rims(0)
     first_half(1)
 
+    @pl.when(third)
+    def _():
+        for d in (1, 2, 3):
+            relay_values(2, d)
+        relay_all_keys(2)
+        first_half(2)
+
     loads[7].wait()
     docs = lens.shape[1]
+
+    def send_edge():
+        remote(edge, edge_in, e_sem.at[0], e_sem.at[1], before).start()
 
     def short_documents():
         for part in range(2):
@@ -442,7 +472,7 @@
             return 0
 
         lax.fori_loop(0, HEADS // WAVE, short_step, 0)
-        remote(edge, edge_in, e_sem.at[0], e_sem.at[1], before).start()
+        pl.when(jnp.logical_not(is_first))(lambda: send_edge())
         pltpu.make_async_copy(so, sout, o_s.at[0]).start()
 
     def document_begins(first_query, queries):
@@ -495,13 +525,6 @@
     short_documents()
     pl.when(par == 1)(lambda: later_step(0))
 
-    @pl.when(third)
-    def _():
-        for d in (1, 2, 3):
-            relay_values(2, d)
-        relay_all_keys(2)
-        first_half(2)
-
     pl.when(par == 0)(lambda: earlier_step(0))
     meet(1)
 
@@ -516,7 +539,7 @@
             for d in range(4):
                 await_bytes(w.at[1, part, pl.ds(0, STRIP)], f_r.at[part, d])
 
-    await_bytes(edge_in, e_sem.at[1])
+    pl.when(jnp.logical_not(is_last))(lambda: await_bytes(edge_in, e_sem.at[1]))
     next_begin = document_begins((c + 1) * ROWS, ROWS)[1]
     last_pos = c * ROWS + ROWS - DOC_MAX + lax.broadcasted_iota(jnp.int32, (DOC_MAX, DOC_MAX), 0)
     reached = last_pos >= next_begin[:, :DOC_MAX]
@@ -657,7 +680,7 @@
         def _():
             await_bytes(hops.at[part, 1], f_s.at[part])
 
-    await_bytes(edge, e_sem.at[0])
+    pl.when(jnp.logical_not(is_first))(lambda: await_bytes(edge, e_sem.at[0]))
     await_bytes(so, o_s.at[0])
     await_bytes(r.at[0], o_s.at[1])
     await_bytes(r.at[3], o_s.at[2])

time: 66.8 us -> 63.7 us (0.954)
  the two profiles are of different devices: /device:TPU:1 before, /device:TPU:25 now
where the time goes in v3:
time: 63.7 us; the launch traced here: 63.5 us
  Pallas kernels  62.9 us (99%)
  between operations  0.64 us (1%)
    pallas_call x1, Pallas kernels, on_device(): pl.pallas_call(kernel, out_shape=shapes, in_specs=[anywhere] * 6, out_spe...  60 us
    pallas_call x1, Pallas kernels, on_device(): pl.pallas_call(hand_over, grid=(LOCAL // PIECE,), out_shape=shapes, in_sp...  2.91 us

profile of v3, /device:TPU:25, one launch (start us, length us, event | category | flops | bytes accessed | tf_op | source)
XLA Modules:
  0.0 63.5 jit_solution(10002219631142945257)
XLA Ops:
  0.6 60.0 %shard_map.93 = (bf16[128,1280]{1,0:T(8,128)(2,1)}, bf16[3,128,1280]{2,1,0:T(8,128)(2,1)}, bf16[128,1280]{1,0:T(8,128)(2,1)}, bf16[3,128,1280]{2,1,0:T(8,128)(2,1)}) custom-call(bf16[3,128,1280]{2,1,0:T(8,128)(2,1)} %lqkv.1, bf16[128,1280]{1,0:T(8,128)(2,1)} %lgrad.1, bf16[3,128,1280]{2,1,0:T(8,128)(2,1)} %sqkv.1, bf16[128,1280]{1,0:T(8,128)(2,1)} %sgrad.1, ...), custom_call_target="tpu_custom_call" | custom-call | tf_op jit(solution)/shard_map/pallas_call | solution.py:709
  60.6 2.9 %shard_map.94 = (bf16[128,1280]{1,0:T(8,128)(2,1)}, bf16[3,128,1280]{2,1,0:T(8,128)(2,1)}, bf16[128,1280]{1,0:T(8,128)(2,1)}, bf16[3,128,1280]{2,1,0:T(8,128)(2,1)}) custom-call(bf16[128,1280]{1,0:T(8,128)(2,1)} %get-tuple-element.8.a, bf16[3,128,1280]{2,1,0:T(8,128)(2,1)} %get-tuple-element.9.b, bf16[128,1280]{1,0:T(8,128)(2,1)} %get-tuple-element.10.c, ...), custom_call_target="tpu_custom_call" | custom-call | tf_op jit(solution)/shard_map/pallas_call | solution.py:764

commit v4 on v3

--- a/solution.py
+++ b/solution.py
@@ -60,7 +60,7 @@
     return lax.fori_loop(0, HEADS // WAVE, group, carry)
 
 
-def attend(items):
+def attend(items, on_stats=None):
     scores = []
     for q, _, pieces in items:
         row = []
@@ -96,6 +96,8 @@
         jnp.sum(do.astype(F32).T * out_t.astype(F32), axis=0, keepdims=True)
         for (_, do, _), out_t in zip(items, outs_t)
     ]
+    if on_stats is not None:
+        on_stats(outs, log_totals, row_dots)
     grads = [
         [(one * (slope - row_dot)).astype(BF16) for one, slope in zip(row, slope_row)]
         for row, slope_row, row_dot in zip(probs, slopes, row_dots)
@@ -194,11 +196,21 @@
             ).start()
 
     def send_values(s, d):
-        for kind, src in ((0, lqkv.at[2]), (1, lgrad)):
+        def send(kind, src):
             remote(
                 src.at[:, columns(first_head(x_at(d), core) + s)], t.at[s, 2 + kind, mine],
                 v_s.at[kind, s, d], v_r.at[kind, s, d], x_dev(d),
             ).start()
+
+        return send
+
+    def send_raw(s):
+        for turn in range(2):
+            for kind, src in ((0, lqkv.at[2]), (1, lgrad)):
+
+                @pl.when(par == (kind + turn) % 2)
+                def _():
+                    to_peers(s, lambda s, d: send_values(s, d)(kind, src))
 
     def send_keys(s, d):
         remote(
@@ -233,7 +245,7 @@
 
     pl.semaphore_wait(barrier, len(peers) + jnp.where(leaves | enters, 1, 0))
 
-    to_peers(0, send_values)
+    send_raw(0)
 
     base = ROWS * (1 - par)
     ending = x == 3 - 3 * par
@@ -304,18 +316,18 @@
     for copy in loads[5:7]:
         copy.wait()
     send_rims(1)
-    to_peers(1, send_values)
+    send_raw(1)
 
     def relay_values(s, d):
         rows = block_rows(lax.rem(x + 4 - d, 4))
-        await_bytes(t.at[s, 2, rows], v_r.at[0, s, d])
-        await_bytes(t.at[s, 3, rows], v_r.at[1, s, d])
+        await_bytes(t.at[s, 2 + par, rows], v_r.at[par, s, d])
         remote(t.at[s, 2 + par, rows], z.at[s, 0, rows], z_s.at[0, s, d], z_r.at[0, s, d], mate).start()
 
     def relay_keys(s, d):
         rows = block_rows(lax.rem(x + 4 - d, 4))
         await_bytes(t.at[s, pl.ds(0, 2), rows], q_r.at[s, d])
         remote(t.at[s, 1 - par, rows], z.at[s, 1, rows], z_s.at[1, s, d], z_r.at[1, s, d], mate).start()
+        await_bytes(t.at[s, 3 - par, rows], v_r.at[1 - par, s, d])
 
     relay_values(0, 0)
     relay_values(1, 0)
@@ -366,7 +378,7 @@
     pl.when(third)(lambda: own_keys(2))
     to_peers(0, send_keys)
     to_peers(1, send_keys)
-    to_peers(2, send_values)
+    send_raw(2)
     to_peers(2, send_keys)
     cross_rims(1)
     for d in (1, 2, 3):
@@ -397,13 +409,18 @@
             (*pair[0], [*early, (k_low, v_low, diag)]),
             (*pair[1], [*early, (k_low, v_low, None), (t[s, 1, high], t[s, 2, high], diag)]),
         ]
-        outs, dqs, log_totals, row_dots, weights, grads = attend(items)
+
+        def tell(_, log_totals, row_dots):
+            for i, rows in enumerate((low, high)):
+                stats[s, 0:1, rows] = log_totals[i]
+                stats[s, 1:2, rows] = row_dots[i]
+            remote(stats.at[s], stats_in.at[s], l_s.at[s], l_r.at[s], mate).start()
+
+        outs, dqs, _, _, weights, grads = attend(items, tell if keep else None)
         for i, rows in enumerate((low, high)):
             g[s, 0, rows] = outs[i]
             g[s, 1, rows] = dqs[i].astype(BF16)
-            if keep:
-                stats[s, 0:1, rows] = log_totals[i]
-                stats[s, 1:2, rows] = row_dots[i]
+        send_back(s, 0)
         at = len(early)
         acc[s, 0, low] = dot(grads[0][at], pair[0][0]) + dot(grads[1][at], pair[1][0])
         acc[s, 1, low] = dot(weights[0][at], pair[0][1]) + dot(weights[1][at], pair[1][1])
@@ -414,7 +431,6 @@
         @pl.when(par == 0)
         def _():
             within(s, [], False)
-            send_back(s, 0)
 
     def relay_all_keys(s):
         for d in range(4):
@@ -501,8 +517,6 @@
     def later_step(s):
         await_mate(s)
         within(s, [(z[s, 1], z[s, 0], None)], True)
-        remote(stats.at[s], stats_in.at[s], l_s.at[s], l_r.at[s], mate).start()
-        send_back(s, 0)
         put_key_grads(s)
 
     def earlier_step(s):
@@ -527,6 +541,8 @@
 
     pl.when(par == 0)(lambda: earlier_step(0))
     meet(1)
+
+    pl.when(third)(lambda: meet(2))
 
     for part in range(2):
 
@@ -607,9 +623,6 @@
         sweep(final_step, 0)
 
     start_inner(1, short_sums)
-    pl.when(third)(lambda: meet(2))
-    end_inner(1, 2, lambda i, cols: sd[i, :, cols])
-    pltpu.make_async_copy(fin.at[pl.ds(2, 2)], sdqkv.at[pl.ds(0, 2)], o_s.at[5]).start()
 
     def await_back(pair, s, d):
         await_bytes(r.at[pl.ds(2 * pair, 2), :, columns(0)], b_r.at[pair, s, d])
@@ -634,8 +647,8 @@
 
     long_sums = sweep(inner_step, (zero, zero))
     start_inner(2, long_sums)
-    end_inner(2, 0, lambda i, cols: r[1 + i, :, cols].astype(F32))
-    pltpu.make_async_copy(fin.at[pl.ds(0, 2)], ldqkv.at[pl.ds(0, 2)], o_s.at[4]).start()
+    end_inner(1, 2, lambda i, cols: sd[i, :, cols])
+    pltpu.make_async_copy(fin.at[pl.ds(2, 2)], sdqkv.at[pl.ds(0, 2)], o_s.at[5]).start()
 
     def left_values(s, d):
         await_bytes(t.at[s, 2, mine], v_s.at[0, s, d])
@@ -656,9 +669,6 @@
         return 0
 
     lax.fori_loop(0, count, left_step, 0)
-    for phase in range(3):
-        for d in (1, 2, 3):
-            await_bytes(sums.at[phase], h_s.at[phase, d])
     for part in range(2):
 
         @pl.when(sends_on)
@@ -685,6 +695,13 @@
     await_bytes(r.at[0], o_s.at[1])
     await_bytes(r.at[3], o_s.at[2])
     await_bytes(fin.at[5], o_s.at[3])
+
+    end_inner(2, 0, lambda i, cols: r[1 + i, :, cols].astype(F32))
+    pltpu.make_async_copy(fin.at[pl.ds(0, 2)], ldqkv.at[pl.ds(0, 2)], o_s.at[4]).start()
+
+    for phase in range(3):
+        for d in (1, 2, 3):
+            await_bytes(sums.at[phase], h_s.at[phase, d])
     await_bytes(fin.at[pl.ds(0, 2)], o_s.at[4])
     await_bytes(fin.at[pl.ds(2, 2)], o_s.at[5])
 

time: 63.7 us -> 62.7 us (0.984)
  Pallas kernels: 62.9 us -> 61.9 us
    pallas_call x1, Pallas kernels: 60 us -> 59 us  [on_device(): pl.pallas_call(kernel, out_shape=shapes, in_specs=[anywhere] * 6, out_spe...]
where the time goes in v4:
time: 62.7 us; the launch traced here: 62.5 us
  Pallas kernels  61.9 us (99%)
  between operations  0.64 us (1%)
    pallas_call x1, Pallas kernels, on_device(): pl.pallas_call(kernel, out_shape=shapes, in_specs=[anywhere] * 6, out_spe...  59 us
    pallas_call x1, Pallas kernels, on_device(): pl.pallas_call(hand_over, grid=(LOCAL // PIECE,), out_shape=shapes, in_sp...  2.91 us

profile of v4, /device:TPU:25, one launch (start us, length us, event | category | flops | bytes accessed | tf_op | source)
XLA Modules:
  0.0 62.5 jit_solution(9739262494160133055)
XLA Ops:
  0.6 59.0 %shard_map.93 = (bf16[128,1280]{1,0:T(8,128)(2,1)}, bf16[3,128,1280]{2,1,0:T(8,128)(2,1)}, bf16[128,1280]{1,0:T(8,128)(2,1)}, bf16[3,128,1280]{2,1,0:T(8,128)(2,1)}) custom-call(bf16[3,128,1280]{2,1,0:T(8,128)(2,1)} %lqkv.1, bf16[128,1280]{1,0:T(8,128)(2,1)} %lgrad.1, bf16[3,128,1280]{2,1,0:T(8,128)(2,1)} %sqkv.1, bf16[128,1280]{1,0:T(8,128)(2,1)} %sgrad.1, ...), custom_call_target="tpu_custom_call" | custom-call | tf_op jit(solution)/shard_map/pallas_call | solution.py:726
  59.6 2.9 %shard_map.94 = (bf16[128,1280]{1,0:T(8,128)(2,1)}, bf16[3,128,1280]{2,1,0:T(8,128)(2,1)}, bf16[128,1280]{1,0:T(8,128)(2,1)}, bf16[3,128,1280]{2,1,0:T(8,128)(2,1)}) custom-call(bf16[128,1280]{1,0:T(8,128)(2,1)} %get-tuple-element.8.a, bf16[3,128,1280]{2,1,0:T(8,128)(2,1)} %get-tuple-element.9.b, bf16[128,1280]{1,0:T(8,128)(2,1)} %get-tuple-element.10.c, ...), custom_call_target="tpu_custom_call" | custom-call | tf_op jit(solution)/shard_map/pallas_call | solution.py:781
